TPU v7x, 256 devices: a whole 4x4x8 slice. The times are simulated.
256 devices in a mesh: seq: 32 (over z, x), head: 8 (over y, core).
Axes of the slice: x: 4, y: 4, z: 8, core: 2. Of those that a mesh axis runs over, the one named last changes fastest.
Arguments:
- queries: bfloat16 [2, 16384, 4096], P(None, 'seq', 'head'), may hold values from -50 to 50
- keys: bfloat16 [2, 16384, 1024], P(None, 'seq', 'head'), may hold values from -6 to 6
- values: bfloat16 [2, 16384, 1024], P(None, 'seq', 'head'), may hold values from -6 to 6
- selected: int32 [2, 32, 32, 3], P(None, 'seq', 'head'), may hold values from 0 to 63, as said below
- length: int32 [1], replicated, may hold values from 16384 to 32768
- out_weight: bfloat16 [4096, 4096], P('head'), may hold values from -0.09375 to 0.09375
Outputs:
- attended: bfloat16 [2, 16384, 4096], P(None, 'seq', 'head')
- projected: bfloat16 [2, 16384, 4096], P(None, ('seq', 'head'))
Inputs may be any that keep to these rules, and one draw needn't show every extreme that they name: `selected`: entry [r, s, h, j] belongs to query block b = r * 32 + s. It is an earlier block, or b itself, which selects no block. The earlier blocks among a head's 3 entries are distinct. For each s and each aligned group of 4 heads, over all r, those heads and j, at most 1 entries name earlier blocks of one same residue modulo 32.
All inputs are finite; a program needn't handle non-finite values.
Results may differ from a plain program's by a relative error of at most 0.02.
Values may be sent and summed in bfloat16 or wider, within the bound.
A program may use at most 128 MiB of HBM per device.

v0:
```python
import jax
import jax.numpy as jnp
from jax import lax
from jax.sharding import PartitionSpec as P

HEAD = 128


def tile_attention(query_tile, key_tile, value_tile, causal_mask):
    scores = jnp.einsum(
        "qd,kd->qk", query_tile, key_tile, preferred_element_type=jnp.float32
    ) * HEAD ** (-0.5)
    scores = jnp.where(causal_mask, scores, -1e30)
    row_max = jnp.max(scores, axis=-1)
    weights = jnp.exp(scores - row_max[:, None])
    row_sum = jnp.sum(weights, axis=-1)
    mixed_rows = jnp.dot(
        weights.astype(jnp.bfloat16), value_tile, preferred_element_type=jnp.float32
    )
    return ((mixed_rows / row_sum[:, None]).astype(jnp.bfloat16), row_max, row_sum)


def merge_parts(own_u, own_m, own_l, far_u, far_m, far_l, usable):
    usable_rows = usable[:, :, None]
    far_safe = jnp.where(usable_rows, far_m, own_m[:, None, :])
    highest = jnp.maximum(own_m, jnp.max(far_safe, axis=1))
    own_weight = own_l * jnp.exp(own_m - highest)
    far_weight = jnp.where(
        usable_rows, far_l * jnp.exp(far_safe - highest[:, None, :]), jnp.float32(0.0)
    )
    weighted = own_weight[..., None] * own_u.astype(jnp.float32)
    weighted = weighted + jnp.sum(far_weight[..., None] * far_u.astype(jnp.float32), axis=1)
    return weighted / (own_weight + jnp.sum(far_weight, axis=1))[..., None]


def per_device(queries, keys, values, selected, length, out_weight):
    rounds, block_len, row_width = queries.shape
    q_heads = row_width // HEAD
    kv_heads = keys.shape[2] // HEAD
    group_size = q_heads // kv_heads
    top_count = selected.shape[3]
    peer_count = lax.axis_size("seq")
    my_seq = lax.axis_index("seq")
    requests = rounds * q_heads * top_count
    capacity = -(-requests // peer_count)
    slot_count = peer_count * capacity
    query_tiles = (
        queries.reshape(rounds, block_len, q_heads, HEAD)
        .transpose(0, 2, 1, 3)
        .reshape(rounds * q_heads, block_len, HEAD)
    )
    key_tiles = (
        keys.reshape(rounds, block_len, kv_heads, HEAD)
        .transpose(0, 2, 1, 3)
        .reshape(rounds * kv_heads, block_len, HEAD)
    )
    value_tiles = (
        values.reshape(rounds, block_len, kv_heads, HEAD)
        .transpose(0, 2, 1, 3)
        .reshape(rounds * kv_heads, block_len, HEAD)
    )
    causal = lax.broadcasted_iota(jnp.int32, (block_len, block_len), 0) >= lax.broadcasted_iota(
        jnp.int32, (block_len, block_len), 1
    )
    own_keys = jnp.broadcast_to(
        key_tiles.reshape(rounds, kv_heads, 1, block_len, HEAD),
        (rounds, kv_heads, group_size, block_len, HEAD),
    ).reshape(rounds * q_heads, block_len, HEAD)
    own_values = jnp.broadcast_to(
        value_tiles.reshape(rounds, kv_heads, 1, block_len, HEAD),
        (rounds, kv_heads, group_size, block_len, HEAD),
    ).reshape(rounds * q_heads, block_len, HEAD)
    own_u, own_m, own_l = jax.vmap(tile_attention, in_axes=(0, 0, 0, None))(
        query_tiles, own_keys, own_values, causal
    )
    chosen = selected.reshape(requests)
    request_order = jnp.arange(requests, dtype=jnp.int32)
    round_of = request_order // (q_heads * top_count)
    head_of = request_order // top_count % q_heads
    usable = chosen < round_of * peer_count + my_seq
    target = chosen % peer_count
    key_index = chosen // peer_count * kv_heads + head_of // group_size
    earlier = (
        (target[:, None] == target[None, :])
        & usable[None, :]
        & (request_order[None, :] < request_order[:, None])
    )
    slot_rank = jnp.sum(earlier, axis=1)
    slot_index = target * capacity + slot_rank
    request_slot = jnp.where(usable, slot_index, 0)
    placed = (slot_index[:, None] == jnp.arange(slot_count, dtype=jnp.int32)[None, :]) & usable[
        :, None
    ]
    filled = jnp.any(placed, axis=0)
    slot_request = jnp.sum(jnp.where(placed, request_order[:, None], 0), axis=0)
    slot_tile = jnp.where(filled, slot_request // top_count, 0)
    slot_key = jnp.where(filled, jnp.sum(jnp.where(placed, key_index[:, None], 0), axis=0), -1)
    outgoing = query_tiles[slot_tile].reshape(peer_count, capacity, block_len, HEAD)
    wanted = slot_key.reshape(peer_count, capacity)
    asked = lax.all_to_all(outgoing, "seq", split_axis=0, concat_axis=0, tiled=True)
    asked_keys = lax.all_to_all(wanted, "seq", split_axis=0, concat_axis=0, tiled=True)
    senders, count_each = asked_keys.shape

    def one_slot(slot_item):
        query_tile, tile_number = slot_item
        return tile_attention(query_tile, key_tiles[tile_number], value_tiles[tile_number], True)

    served_u, served_m, served_l = lax.map(
        one_slot,
        (
            asked.reshape(senders * count_each, block_len, HEAD),
            jnp.maximum(asked_keys.reshape(-1), 0),
        ),
        batch_size=4,
    )
    back_u, back_m, back_l = (
        lax.all_to_all(
            served_u.reshape(senders, count_each, block_len, HEAD),
            "seq",
            split_axis=0,
            concat_axis=0,
            tiled=True,
        ),
        lax.all_to_all(
            served_m.reshape(senders, count_each, block_len),
            "seq",
            split_axis=0,
            concat_axis=0,
            tiled=True,
        ),
        lax.all_to_all(
            served_l.reshape(senders, count_each, block_len),
            "seq",
            split_axis=0,
            concat_axis=0,
            tiled=True,
        ),
    )
    far_u = back_u.reshape(slot_count, block_len, HEAD)[request_slot]
    far_m = back_m.reshape(slot_count, block_len)[request_slot]
    far_l = back_l.reshape(slot_count, block_len)[request_slot]
    tile_total = rounds * q_heads
    merged = merge_parts(
        own_u,
        own_m,
        own_l,
        far_u.reshape(tile_total, top_count, block_len, HEAD),
        far_m.reshape(tile_total, top_count, block_len),
        far_l.reshape(tile_total, top_count, block_len),
        usable.reshape(tile_total, top_count),
    )
    position = ((jnp.arange(rounds, dtype=jnp.int32) * peer_count + my_seq) * block_len)[
        :, None
    ] + jnp.arange(block_len, dtype=jnp.int32)[None, :]
    live_rows = position < length[0]
    merged = merged.reshape(rounds, q_heads, block_len, HEAD)
    merged = jnp.where(live_rows[:, None, :, None], merged, jnp.float32(0.0)).astype(jnp.bfloat16)
    attended = merged.transpose(0, 2, 1, 3).reshape(rounds, block_len, row_width)
    token_rows = attended.transpose(1, 0, 2).reshape(block_len * rounds, row_width)
    summed = lax.psum_scatter(
        jnp.dot(token_rows, out_weight, preferred_element_type=jnp.float32).astype(jnp.bfloat16),
        "head",
        scatter_dimension=0,
        tiled=True,
    ).astype(jnp.float32)
    mine = summed.shape[0] // rounds
    projected = (
        summed.reshape(mine, rounds, summed.shape[1]).transpose(1, 0, 2).astype(jnp.bfloat16)
    )
    return (attended, projected)


def solution(mesh):
    placed = (
        P(None, "seq", "head"),
        P(None, "seq", "head"),
        P(None, "seq", "head"),
        P(None, "seq", "head", None),
        P(),
        P("head", None),
    )
    return jax.shard_map(
        per_device,
        mesh=mesh,
        in_specs=placed,
        out_specs=(P(None, "seq", "head"), P(None, ("seq", "head"), None)),
        check_vma=False,
    )
```

profile of v0, /device:TPU:1, one launch (start us, length us, event | category | flops | bytes accessed | tf_op | source)
XLA Modules:
  0.0 423.6 jit_solution(5829713494863365672)
XLA Ops:
  9.2 11.9 %all-to-all-start.1 = ((s32[32,1,1]{2,1,0:T(1,128)}), s32[32,1,1]{2,1,0:T(1,128)S(1)}, u32[]{:S(2)}, u32[]{:S(2)}) async-start(s32[32,1,1]{2,1,0:T(1,128)} %copy.59), calls=%async_computation.1 | async-start | bytes 32768 | tf_op jit(solution)/shard_map/all_to_all | solution.py:101
  21.1 1.3 fusion.55
  22.5 3.1 gather_fusion.2
  25.5 4.0 all-to-all-done.1
  29.6 5.4 %all-to-all-start = ((bf16[32,1,512,128]{3,2,1,0:T(8,128)(2,1)}), bf16[32,1,512,128]{3,2,1,0:T(8,128)(2,1)}, u32[]{:S(2)}, u32[]{:S(2)}) async-start(bf16[32,1,512,128]{3,2,1,0:T(8,128)(2,1)} %bitcast.107), calls=%async_computation | async-start | bytes 8388608 | tf_op jit(solution)/shard_map/all_to_all | solution.py:100
  36.1 91.0 %all-to-all-done = bf16[32,1,512,128]{3,2,1,0:T(8,128)(2,1)} async-done(((bf16[32,1,512,128]{3,2,1,0:T(8,128)(2,1)}), bf16[32,1,512,128]{3,2,1,0:T(8,128)(2,1)}, u32[]{:S(2)}, u32[]{:S(2)}) %all-to-all-start) | async-done | bytes 4194336 | tf_op jit(solution)/shard_map/all_to_all | solution.py:100
  127.1 78.6 %while.14 = (s32[]{:T(128)}, bf16[8,4,512,128]{3,2,1,0:T(8,128)(2,1)}, f32[8,4,512]{2,1,0:T(4,128)S(1)}, f32[8,4,512]{2,1,0:T(4,128)S(1)}, bf16[8,4,512,128]{3,2...) while((s32[]{:T(128)}, ...), condition=%wide.region_9.10_spmd, body=%wide.region_6.9_spmd.sunk | while | flops 545779712 | bytes 33629440 | solution.py:108
  127.7 1.8 multiply_reduce_fusion.2
  129.5 2.0 copy-done
  132.8 4.1 fusion.72
  137.6 1.8 multiply_reduce_fusion.2
  139.4 2.0 copy-done
  142.6 4.2 fusion.72
  147.4 1.8 multiply_reduce_fusion.2
  149.2 2.0 copy-done
  152.5 4.1 fusion.72
  157.2 1.8 multiply_reduce_fusion.2
  159.0 2.0 copy-done
  162.3 4.1 fusion.72
  167.0 1.8 multiply_reduce_fusion.2
  168.9 2.0 copy-done
  172.1 4.1 fusion.72
  176.9 1.8 multiply_reduce_fusion.2
  178.7 2.0 copy-done
  182.0 4.1 fusion.72
  186.7 1.8 multiply_reduce_fusion.2
  188.5 2.0 copy-done
  191.8 4.1 fusion.72
  196.5 1.8 multiply_reduce_fusion.2
  198.3 2.0 copy-done
  201.6 4.1 fusion.72
  206.5 8.3 %all-to-all-start.2 = ((f32[32,1,512]{2,1,0:T(1,128)}), f32[32,1,512]{2,1,0:T(1,128)S(1)}, u32[]{:S(2)}, u32[]{:S(2)}) async-start(f32[32,1,512]{2,1,0:T(1,128)} %reshape_reshape.13), calls=%async_computation.2 | async-start | bytes 131072 | tf_op jit(solution)/shard_map/all_to_all | solution.py:124
  214.9 8.7 %all-to-all-done.2 = f32[32,1,512]{2,1,0:T(1,128)S(1)} async-done(((f32[32,1,512]{2,1,0:T(1,128)}), f32[32,1,512]{2,1,0:T(1,128)S(1)}, u32[]{:S(2)}, u32[]{:S(2)}) %all-to-all-start.2) | async-done | bytes 65568 | tf_op jit(solution)/shard_map/all_to_all | solution.py:124
  223.6 11.9 %all_to_all.26 = f32[32,1,512]{2,1,0:T(1,128)S(1)} all-to-all(f32[32,1,512]{2,1,0:T(1,128)S(1)} %reshape_reshape.14), channel_id=1, replica_groups=mesh['seq'=32,'head'=8] {'seq'}, dimensions={0} | all-to-all | bytes 131072 | tf_op jit(solution)/shard_map/all_to_all | solution.py:131
  235.5 5.0 %all-to-all-start.4 = ((bf16[32,1,512,128]{3,2,1,0:T(8,128)(2,1)}), bf16[32,1,512,128]{3,2,1,0:T(8,128)(2,1)}, u32[]{:S(2)}, u32[]{:S(2)}) async-start(bf16[32,1,512,128]{3,2,1,0:T(8,128)(2,1)} %bitcast.111), calls=%async_computation.4 | async-start | bytes 8388608 | tf_op jit(solution)/shard_map/all_to_all | solution.py:117
  242.1 1.5 fusion.24
  243.6 1.7 fusion.26
  245.4 1.5 copy-done.1
  248.4 82.8 %all-to-all-done.4 = bf16[32,1,512,128]{3,2,1,0:T(8,128)(2,1)} async-done(((bf16[32,1,512,128]{3,2,1,0:T(8,128)(2,1)}), bf16[32,1,512,128]{3,2,1,0:T(8,128)(2,1)}, u32[]{:S(2)}, u32[]{:S(2)}) %all-to-all-start.4) | async-done | bytes 4194336 | tf_op jit(solution)/shard_map/all_to_all | solution.py:117
  331.2 3.3 gather_fusion.5
  334.5 3.4 fusion.27
  338.0 2.0 copy.65
  340.0 6.0 %add_divide_fusion = bf16[8,512,128]{1,2,0:T(8,128)(2,1)S(1)} fusion(f32[8,512,128]{1,2,0:T(8,128)S(1)} %copy.65, f32[8,512]{1,0:T(8,128)S(1)} %get-tuple-element.99, f32[8,512]{1,0:T(8,128)S(1)} %fusion.26, f32[8,512]{1,0:T(8,128)S(1)} %get-tuple-element.100, bf16[8,512,128]{1,2,0:T(8,128)(2,1)S(1)} %bitcast.116, f32[8,512,512]{1,2,0:T(8,128)} %copy-done.1, ...), kind=kOutput, calls=%fused_computation.42 | convolution fusion | flops 548929536 | bytes 12910592 | tf_op jit(solution)/shard_map/vmap()/dot_general | solution.py:17
  347.7 8.9 %convolution_convert_fusion = bf16[1024,4096]{1,0:T(8,128)(2,1)} fusion(bf16[1024,512]{1,0:T(8,128)(2,1)S(1)} %reshape.520, bf16[512,4096]{1,0:T(8,128)(2,1)} %param.13), kind=kOutput, calls=%fused_computation.30 | convolution fusion | flops 4299161600 | bytes 13631488 | tf_op jit(solution)/shard_map/dot_general | solution.py:161
  356.6 1.3 copy.73
  357.9 55.5 %reduce-scatter.2.cloned.1.call-done = bf16[128,4096]{1,0:T(8,128)(2,1)} async-done(((bf16[1024,4096]{1,0:T(8,128)(2,1)}), bf16[128,4096]{1,0:T(8,128)(2,1)}) %reduce-scatter.2.cloned.1.call-update) | async-done | bytes 1048592 | tf_op jit(solution)/shard_map/reduce_scatter | solution.py:160
  413.4 1.7 convert_element_type.46
  415.2 1.6 copy.80
  (108 shorter events, 23.2 us)
Async XLA Ops:
  9.2 20.4 %all-to-all-start.1 = ((s32[32,1,1]{2,1,0:T(1,128)}), s32[32,1,1]{2,1,0:T(1,128)S(1)}, u32[]{:S(2)}, u32[]{:S(2)}) async-start(s32[32,1,1]{2,1,0:T(1,128)} %copy.59), calls=%async_computation.1 | async-start | bytes 32768 | tf_op jit(solution)/shard_map/all_to_all | solution.py:101
  29.6 5.5 %copy-start.5 = (bf16[2,512,128]{2,1,0:T(8,128)(2,1)S(1)}, bf16[2,512,128]{2,1,0:T(8,128)(2,1)}, u32[]{:S(2)}) copy-start(bf16[2,512,128]{2,1,0:T(8,128)(2,1)} %param.10) | copy-start | bytes 786436
  29.6 5.6 %copy-start.4 = (bf16[2,512,128]{2,1,0:T(8,128)(2,1)S(1)}, bf16[2,512,128]{2,1,0:T(8,128)(2,1)}, u32[]{:S(2)}) copy-start(bf16[2,512,128]{2,1,0:T(8,128)(2,1)} %param.9) | copy-start | bytes 786436
  29.6 97.5 %all-to-all-start = ((bf16[32,1,512,128]{3,2,1,0:T(8,128)(2,1)}), bf16[32,1,512,128]{3,2,1,0:T(8,128)(2,1)}, u32[]{:S(2)}, u32[]{:S(2)}) async-start(bf16[32,1,512,128]{3,2,1,0:T(8,128)(2,1)} %bitcast.107), calls=%async_computation | async-start | bytes 8388608 | tf_op jit(solution)/shard_map/all_to_all | solution.py:100
  129.5 2.0 copy-start
  139.4 2.0 copy-start
  149.2 2.0 copy-start
  159.0 2.0 copy-start
  168.9 2.0 copy-start
  178.7 2.0 copy-start
  188.5 2.0 copy-start
  198.3 2.0 copy-start
  206.5 17.1 %all-to-all-start.2 = ((f32[32,1,512]{2,1,0:T(1,128)}), f32[32,1,512]{2,1,0:T(1,128)S(1)}, u32[]{:S(2)}, u32[]{:S(2)}) async-start(f32[32,1,512]{2,1,0:T(1,128)} %reshape_reshape.13), calls=%async_computation.2 | async-start | bytes 131072 | tf_op jit(solution)/shard_map/all_to_all | solution.py:124
  235.5 5.3 %copy-start.6 = (s32[2,1,4,3]{2,1,3,0:T(1,128)S(1)}, s32[2,1,4,3]{2,1,3,0:T(1,128)}, u32[]{:S(2)}) copy-start(s32[2,1,4,3]{2,1,3,0:T(1,128)} %param.11) | copy-start | bytes 292
  235.5 95.7 %all-to-all-start.4 = ((bf16[32,1,512,128]{3,2,1,0:T(8,128)(2,1)}), bf16[32,1,512,128]{3,2,1,0:T(8,128)(2,1)}, u32[]{:S(2)}, u32[]{:S(2)}) async-start(bf16[32,1,512,128]{3,2,1,0:T(8,128)(2,1)} %bitcast.111), calls=%async_computation.4 | async-start | bytes 8388608 | tf_op jit(solution)/shard_map/all_to_all | solution.py:117
  240.5 172.9 %reduce-scatter.2.cloned.1.call-start = ((), (), s32[]{:S(2)}) async-start(), calls=%async_computation.6 | async-start | bytes 9437184 | tf_op jit(solution)/shard_map/reduce_scatter | solution.py:160
  241.8 1.8 copy-start.2
  243.6 3.2 copy-start.1
  338.0 2.1 copy-start.3
Sparse Core Ops, SparseCore 0:
  356.7 56.6 reduce-scatter.1
where the time goes:
time: 425 us; the launch traced here: 424 us
  waiting for transfers between devices  242 us (57%)
  matrix products  63.9 us (15%)
  local copies, waits for them, and re-layouts  46.8 us (11%)
  starting transfers between devices  30.8 us (7%)
  between operations  15 us (4%)
  other arithmetic  12.7 us (3%)
  blocking collectives  11.9 us (3%)
    all_to_all x1, waiting for transfers between devices, per_device(): lax.all_to_all(outgoing, 'seq', split_axis=0, concat_axis=0, tiled=True)  91 us
    all_to_all x1, waiting for transfers between devices, per_device(): lax.all_to_all(served_u.reshape(senders, count_each, block_len, HEAD), 's...  82.8 us
    reduce_scatter x1, waiting for transfers between devices, per_device(): lax.psum_scatter(jnp.dot(token_rows, out_weight, preferred_element_type=j...  55.5 us
    dot_general x9, matrix products, tile_attention(): jnp.dot(weights.astype(jnp.bfloat16), value_tile, preferred_element_type=...  39 us
    dot_general x9, matrix products, tile_attention(): jnp.einsum('qd,kd->qk', query_tile, key_tile, preferred_element_type=jnp....  16 us
    while x16, local copies, waits for them, and re-layouts  15.7 us
    all_to_all x1, blocking collectives, per_device(): lax.all_to_all(served_l.reshape(senders, count_each, block_len), 'seq', s...  11.9 us
    all_to_all x1, starting transfers between devices, per_device(): lax.all_to_all(wanted, 'seq', split_axis=0, concat_axis=0, tiled=True)  11.9 us
  transfers between devices with their start and end apart: 5, of which 5 were waited for; matrix products, arithmetic and copies ran while one was open for 3% of the time, Pallas kernels for 0%

commit v1 on v0

v1 whole, which is shorter than its diff:
```python
import functools

import jax
import jax.numpy as jnp
from jax import lax
from jax.experimental import pallas as pl
from jax.experimental.pallas import tpu as pltpu
from jax.sharding import PartitionSpec as P

HEAD = 128
SCALE = HEAD ** (-0.5)
LOG2E = 1.4426950408889634


def tile_scores(key_tile, query_tile):
    return lax.dot_general(
        key_tile, query_tile, (((1,), (1,)), ((), ())), preferred_element_type=jnp.float32
    )


def attention_kernel(
    top_count, block_of, usable_of, live, q_ref, k_ref, v_ref, fk_ref, fv_ref, o_ref, top, total, acc
):
    head = pl.program_id(0)
    slot = pl.program_id(1)
    block_len = q_ref.shape[0]

    @pl.when(slot == 0)
    def _():
        scores = tile_scores(k_ref[...], q_ref[...])
        key_at = lax.broadcasted_iota(jnp.int32, scores.shape, 0)
        query_at = lax.broadcasted_iota(jnp.int32, scores.shape, 1)
        scores = jnp.where(key_at <= query_at, scores, -1e30)
        highest = jnp.max(scores, axis=0, keepdims=True)
        weights = jnp.exp2((scores - highest) * (SCALE * LOG2E))
        top[...] = highest
        total[...] = jnp.sum(weights, axis=0, keepdims=True)
        acc[...] = lax.dot_general(
            v_ref[...],
            weights.astype(jnp.bfloat16),
            (((0,), (0,)), ((), ())),
            preferred_element_type=jnp.float32,
        )

    @pl.when(usable_of[head * top_count + slot] != 0)
    def _():
        scores = tile_scores(fk_ref[0, 0], q_ref[...])
        before = top[...]
        highest = jnp.maximum(before, jnp.max(scores, axis=0, keepdims=True))
        shrink = jnp.exp2((before - highest) * (SCALE * LOG2E))
        weights = jnp.exp2((scores - highest) * (SCALE * LOG2E))
        top[...] = highest
        total[...] = total[...] * shrink + jnp.sum(weights, axis=0, keepdims=True)
        acc[...] = acc[...] * shrink + lax.dot_general(
            fv_ref[0, 0],
            weights.astype(jnp.bfloat16),
            (((0,), (0,)), ((), ())),
            preferred_element_type=jnp.float32,
        )

    @pl.when(slot == top_count - 1)
    def _():
        rows = lax.broadcasted_iota(jnp.int32, (1, block_len), 1)
        mixed = jnp.where(rows < live[0], acc[...] / total[...], 0.0)
        o_ref[...] = mixed.T.astype(jnp.bfloat16)


def attend(queries, keys, values, far, round_now, chosen, usable, live):
    block_len, row_width = queries.shape
    heads = row_width // HEAD
    top_count = chosen.shape[1]
    members = far.shape[1] // 2
    chosen = chosen.reshape(-1)

    def far_map(part, head, slot, block_of, usable_of, live):
        block = block_of[head * top_count + slot]
        return (block % 32, block // 32 * 2 + part, 0, 0)

    return pl.pallas_call(
        functools.partial(attention_kernel, top_count),
        grid_spec=pltpu.PrefetchScalarGridSpec(
            num_scalar_prefetch=3,
            grid=(heads, top_count),
            in_specs=[
                pl.BlockSpec((block_len, HEAD), lambda h, j, *_: (0, h)),
                pl.BlockSpec((block_len, HEAD), lambda h, j, *_: (0, 0)),
                pl.BlockSpec((block_len, HEAD), lambda h, j, *_: (0, 0)),
                pl.BlockSpec((1, 1, block_len, HEAD), functools.partial(far_map, 0)),
                pl.BlockSpec((1, 1, block_len, HEAD), functools.partial(far_map, 1)),
            ],
            out_specs=pl.BlockSpec((block_len, HEAD), lambda h, j, *_: (0, h)),
            scratch_shapes=[
                pltpu.VMEM((1, block_len), jnp.float32),
                pltpu.VMEM((1, block_len), jnp.float32),
                pltpu.VMEM((HEAD, block_len), jnp.float32),
            ],
        ),
        out_shape=jax.ShapeDtypeStruct((block_len, row_width), jnp.bfloat16),
        compiler_params=pltpu.CompilerParams(vmem_limit_bytes=32 * 1024 * 1024),
        cost_estimate=pl.CostEstimate(
            flops=16 * 4 * block_len * block_len * HEAD * 2,
            bytes_accessed=12 * 1024 * 1024,
            transcendentals=16 * block_len * block_len,
        ),
        name=f"attend_{round_now}",
    )(chosen, usable, live, queries, keys, values, far, far)


def per_device(queries, keys, values, selected, length, out_weight):
    rounds, block_len, row_width = queries.shape
    peers = lax.axis_size("seq")
    my_seq = lax.axis_index("seq")
    gathered = [
        lax.all_gather(jnp.stack([keys[r], values[r]]), "seq", axis=0) for r in range(rounds)
    ]
    attended, projected = [], []
    for r in range(rounds):
        block = r * peers + my_seq
        chosen = selected[r, 0]
        usable = (chosen < block).astype(jnp.int32)
        safe = jnp.where(chosen < block, chosen, 0)
        far = gathered[0] if r == 0 else jnp.concatenate(gathered[: r + 1], axis=1)
        live = jnp.reshape(length[0] - block * block_len, (1,))
        rows = attend(
            queries[r], keys[r], values[r], far, r, safe, usable.reshape(-1), live
        )
        attended.append(rows)
        term = jnp.dot(rows, out_weight, preferred_element_type=jnp.float32).astype(jnp.bfloat16)
        projected.append(lax.psum_scatter(term, "head", scatter_dimension=0, tiled=True))
    return jnp.stack(attended), jnp.stack(projected)


def solution(mesh):
    placed = (
        P(None, "seq", "head"),
        P(None, "seq", "head"),
        P(None, "seq", "head"),
        P(None, "seq", "head", None),
        P(),
        P("head", None),
    )
    return jax.shard_map(
        per_device,
        mesh=mesh,
        in_specs=placed,
        out_specs=(P(None, "seq", "head"), P(None, ("seq", "head"), None)),
        check_vma=False,
    )
```

time: 425 us -> 324 us (0.76)
  matrix products: 63.9 us -> 8.73 us
  local copies, waits for them, and re-layouts: 46.8 us -> 6.95 us
  starting transfers between devices: 30.8 us -> 0.16 us
  waiting for transfers between devices: 242 us -> 262 us
  Pallas kernels: 0 us -> 16.3 us
  blocking collectives: 11.9 us -> 0 us
    all_gather x0 -> x2, waiting for transfers between devices: none -> 199 us  [per_device(): lax.all_gather(jnp.stack([keys[r], values[r]]), 'seq', axis=0)]
    all_to_all x4 -> x0, waiting for transfers between devices: 187 us -> none  [the longest x1 91 us: per_device(): lax.all_to_all(outgoing, 'seq', split_axis=0, concat_axis=0, tiled=True)]
    dot_general x19 -> x2, matrix products: 63.9 us -> 8.73 us  [per_device(): jnp.dot(rows, out_weight, preferred_element_type=jnp.float32)]
    all_to_all x4 -> x0, starting transfers between devices: 30.6 us -> none  [the longest x1 11.9 us: per_device(): lax.all_to_all(wanted, 'seq', split_axis=0, concat_axis=0, tiled=True)]
    gather x20 -> x0, local copies, waits for them, and re-layouts: 16.9 us -> none  [the longest x8 4.67 us: one_slot(): value_tiles[tile_number]]
    pallas_call x0 -> x2, Pallas kernels: none -> 16.3 us  [attend(): pl.pallas_call(functools.partial(attention_kernel, top_count), grid_spec=...]
    while x18 -> x0, local copies, waits for them, and re-layouts: 16 us -> none
    all_to_all x1 -> x0, blocking collectives: 11.9 us -> none  [per_device(): lax.all_to_all(served_l.reshape(senders, count_each, block_len), 'seq', s...]
  transfers between devices with their start and end apart: 5 -> 4, of which waited for: 5 -> 4; matrix products, arithmetic and copies ran while one was open for 3% -> 3% of each run, Pallas kernels for 0% -> 1%
where the time goes in v1:
time: 324 us; the launch traced here: 322 us
  waiting for transfers between devices  262 us (81%)
  Pallas kernels  16.3 us (5%)
  between operations  14.5 us (4%)
  other arithmetic  12.8 us (4%)
  matrix products  8.73 us (3%)
  local copies, waits for them, and re-layouts  6.95 us (2%)
    all_gather x2, waiting for transfers between devices, per_device(): lax.all_gather(jnp.stack([keys[r], values[r]]), 'seq', axis=0)  199 us
    reduce_scatter x2, waiting for transfers between devices, per_device(): lax.psum_scatter(term, 'head', scatter_dimension=0, tiled=True)  63.7 us
    pallas_call x2, Pallas kernels, attend(): pl.pallas_call(functools.partial(attention_kernel, top_count), grid_spec=...  16.3 us
    dot_general x2, matrix products, per_device(): jnp.dot(rows, out_weight, preferred_element_type=jnp.float32)  8.73 us
    concatenate x1, other arithmetic, per_device(): far = gathered[0] if r == 0 else jnp.concatenate(gathered[:r + 1], axis=1)  7.97 us
  transfers between devices with their start and end apart: 4, of which 4 were waited for; matrix products, arithmetic and copies ran while one was open for 3% of the time, Pallas kernels for 1%

profile of v1, /device:TPU:1, one launch (start us, length us, event | category | flops | bytes accessed | tf_op | source)
XLA Modules:
  0.0 321.8 jit_solution(6643762998176712876)
XLA Ops:
  7.2 0.0 all-gather.5.cloned.1.call-start
  7.2 1.2 slice_bitcast_fusion.4
  8.4 0.7 pad_maximum_fusion.3
  9.2 0.0 all-gather.5.cloned.1.call-update
  9.2 0.0 all-gather.7.cloned.1.call-start
  9.2 0.7 pad_maximum_fusion.4
  10.0 0.0 all-gather.7.cloned.1.call-update
  10.0 0.0 reduce-scatter.5.cloned.1.call-start
  10.1 0.7 fusion
  10.8 0.1 copy.13
  10.9 0.1 squeeze.33
  11.6 1.3 slice_bitcast_fusion.1
  12.9 100.0 %all-gather.5.cloned.1.call-done = bf16[64,512,128]{2,1,0:T(8,128)(2,1)} async-done(((bf16[2,512,128]{2,1,0:T(8,128)(2,1)}), bf16[64,512,128]{2,1,0:T(8,128)(2,1)}) %all-gather.5.cloned.1.call-update) | async-done | bytes 8388624 | tf_op jit(solution)/shard_map/all_gather | solution.py:114
  112.9 98.6 %all-gather.7.cloned.1.call-done = bf16[64,512,128]{2,1,0:T(8,128)(2,1)} async-done(((bf16[2,512,128]{2,1,0:T(8,128)(2,1)}), bf16[64,512,128]{2,1,0:T(8,128)(2,1)}) %all-gather.7.cloned.1.call-update) | async-done | bytes 8388624 | tf_op jit(solution)/shard_map/all_gather | solution.py:114
  211.5 8.0 %pad_maximum_fusion.fk_ref.fv_ref = bf16[32,4,512,128]{3,2,1,0:T(8,128)(2,1)S(1)} fusion(bf16[32,2,512,128]{3,2,1,0:T(8,128)(2,1)} %bitcast.32, bf16[32,2,512,128]{3,2,1,0:T(8,128)(2,1)} %bitcast.27), kind=kLoop, calls=%fused_computation | loop fusion | flops 8388608 | bytes 33554432 | tf_op jit(solution)/shard_map/concatenate | solution.py:122
  219.5 0.0 copy-start.1
  219.5 12.2 %attend_1.1 = bf16[512,512]{1,0:T(8,128)(2,1)S(1)} custom-call(s32[12]{0:T(128)S(1)} %compare_select_fusion.block_of, s32[12]{0:T(128)S(1)} %compare_convert_fusion.usable_of, s32[1]{0:T(128)} %bitcast.7.live, bf16[512,512]{1,0:T(8,128)(2,1)S(1)} %get-tuple-element.3.q_ref, bf16[512,128]{1,0:T(8,128)(2,1)S(1)} %get-tuple-element.16.k_ref, ...), custom_call_target="tpu_custom_call" | custom-call | flops 4294967296 | bytes 12582912 | tf_op jit(solution)/shard_map/attend_1/pallas_call | solution.py:79
  231.7 0.0 copy-done.1
  231.8 4.4 %convolution_convert_fusion = bf16[512,4096]{1,0:T(8,128)(2,1)} fusion(bf16[512,512]{1,0:T(8,128)(2,1)S(1)} %attend_1.1, bf16[512,4096]{1,0:T(8,128)(2,1)S(1)} %copy-done.1), kind=kOutput, calls=%fused_computation.1 | convolution fusion | flops 2149580800 | bytes 8912896 | tf_op jit(solution)/shard_map/dot_general | solution.py:128
  236.1 0.0 reduce-scatter.5.cloned.1.call-update
  236.1 0.0 reduce-scatter.3.cloned.1.call-start
  236.2 0.1 copy.12
  236.3 0.1 squeeze.28
  236.4 0.0 copy-start
  236.4 3.4 %copy-done = bf16[64,512,128]{2,1,0:T(8,128)(2,1)S(1)} copy-done((bf16[64,512,128]{2,1,0:T(8,128)(2,1)S(1)}, bf16[64,512,128]{2,1,0:T(8,128)(2,1)}, u32[]{:S(2)}) %copy-start) | copy-done | bytes 8388632
  239.8 0.0 copy-start.2
  239.8 4.1 %attend_0.1 = bf16[512,512]{1,0:T(8,128)(2,1)S(1)} custom-call(s32[12]{0:T(128)S(1)} %compare_select_fusion.1.block_of, s32[12]{0:T(128)S(1)} %compare_convert_fusion.1.usable_of, s32[1]{0:T(128)} %bitcast.1.live, bf16[512,512]{1,0:T(8,128)(2,1)S(1)} %get-tuple-element.2.q_ref, bf16[512,128]{1,0:T(8,128)(2,1)S(1)} %get-tuple-element.17.k_ref, ...), custom_call_target="tpu_custom_call" | custom-call | flops 4294967296 | bytes 12582912 | tf_op jit(solution)/shard_map/attend_0/pallas_call | solution.py:79
  243.9 0.0 copy-done.2
  243.9 4.4 %convolution_convert_fusion.1 = bf16[512,4096]{1,0:T(8,128)(2,1)} fusion(bf16[512,512]{1,0:T(8,128)(2,1)S(1)} %attend_0.1, bf16[512,4096]{1,0:T(8,128)(2,1)S(1)} %copy-done.2), kind=kOutput, calls=%fused_computation.2 | convolution fusion | flops 2149580800 | bytes 8912896 | tf_op jit(solution)/shard_map/dot_general | solution.py:128
  248.2 0.0 reduce-scatter.3.cloned.1.call-update
  248.3 1.1 pad_maximum_fusion.1
  249.3 21.9 %reduce-scatter.5.cloned.1.call-done = bf16[64,4096]{1,0:T(8,128)(2,1)} async-done(((bf16[512,4096]{1,0:T(8,128)(2,1)}), bf16[64,4096]{1,0:T(8,128)(2,1)}) %reduce-scatter.5.cloned.1.call-update) | async-done | bytes 524304 | tf_op jit(solution)/shard_map/reduce_scatter | solution.py:129
  271.2 41.8 %reduce-scatter.3.cloned.1.call-done = bf16[64,4096]{1,0:T(8,128)(2,1)} async-done(((bf16[512,4096]{1,0:T(8,128)(2,1)}), bf16[64,4096]{1,0:T(8,128)(2,1)}) %reduce-scatter.3.cloned.1.call-update) | async-done | bytes 524304 | tf_op jit(solution)/shard_map/reduce_scatter | solution.py:129
  313.0 2.3 pad_maximum_fusion.2
  (4 shorter events, 0.0 us)
Async XLA Ops:
  7.2 105.7 %all-gather.5.cloned.1.call-start = ((), (), s32[]{:S(2)}) async-start(), calls=%async_computation.4 | async-start | bytes 8650752 | tf_op jit(solution)/shard_map/all_gather | solution.py:114
  9.2 202.3 %all-gather.7.cloned.1.call-start = ((), (), s32[]{:S(2)}) async-start(), calls=%async_computation.5 | async-start | bytes 8650752 | tf_op jit(solution)/shard_map/all_gather | solution.py:114
  10.0 261.2 %reduce-scatter.5.cloned.1.call-start = ((), (), s32[]{:S(2)}) async-start(), calls=%async_computation.3 | async-start | bytes 4718592 | tf_op jit(solution)/shard_map/reduce_scatter | solution.py:129
  219.5 12.3 %copy-start.1 = (bf16[512,4096]{1,0:T(8,128)(2,1)S(1)}, bf16[512,4096]{1,0:T(8,128)(2,1)}, u32[]{:S(2)}) copy-start(bf16[512,4096]{1,0:T(8,128)(2,1)} %param.11) | copy-start | bytes 12582916
  236.1 76.9 %reduce-scatter.3.cloned.1.call-start = ((), (), s32[]{:S(2)}) async-start(), calls=%async_computation.2 | async-start | bytes 4718592 | tf_op jit(solution)/shard_map/reduce_scatter | solution.py:129
  236.4 3.4 %copy-start = (bf16[64,512,128]{2,1,0:T(8,128)(2,1)S(1)}, bf16[64,512,128]{2,1,0:T(8,128)(2,1)}, u32[]{:S(2)}) copy-start(bf16[64,512,128]{2,1,0:T(8,128)(2,1)} %all-gather.5.cloned.1.call-done) | copy-start | bytes 25165828
  239.8 4.1 %copy-start.2 = (bf16[512,4096]{1,0:T(8,128)(2,1)S(1)}, bf16[512,4096]{1,0:T(8,128)(2,1)}, u32[]{:S(2)}) copy-start(bf16[512,4096]{1,0:T(8,128)(2,1)} %param.11) | copy-start | bytes 12582916
Sparse Core Ops, SparseCore 0:
  11.2 101.6 all-gather.4
  116.0 95.4 all-gather.6
  236.3 34.9 reduce-scatter.4
  273.7 39.3 reduce-scatter.2

commit v2 on v1

v2 whole, which is shorter than its diff:
```python
import jax
import jax.numpy as jnp
from jax import lax
from jax.experimental import pallas as pl
from jax.experimental.pallas import tpu as pltpu
from jax.sharding import PartitionSpec as P

HEAD = 128
Z, X, Y = 8, 4, 4
PEERS = Z * X
BLOCK = 512
HEADS = 4
TOPK = 3
ROUNDS = 2
MODEL = 4096
GAIN = HEAD ** (-0.5) * 1.4426950408889634
CUT = 304
STAGES = 10
COMPUTE_END = (STAGES + 1) * 5 - 1
POST_0 = 34
POST_1 = COMPUTE_END
POST_STEPS = 12
COLS = 1024
HALF = COLS // 2
MESH = pl.DeviceIdType.MESH


def soft_part(key_tile, value_t, query_t, mask_from=None):
    scores = jnp.dot(key_tile, query_t, preferred_element_type=jnp.float32)
    if mask_from is not None:
        key_at = lax.broadcasted_iota(jnp.int32, scores.shape, 0)
        query_at = lax.broadcasted_iota(jnp.int32, scores.shape, 1) + mask_from
        scores = jnp.where(key_at <= query_at, scores, -1e30)
    highest = jnp.max(scores, axis=0, keepdims=True)
    weights = jnp.exp2((scores - highest) * GAIN)
    total = jnp.sum(weights, axis=0, keepdims=True)
    mixed = jnp.dot(value_t, weights.astype(jnp.bfloat16), preferred_element_type=jnp.float32)
    return mixed, highest, total


def value_rows(stacked):
    return jnp.concatenate([stacked[c * HEAD : (c + 1) * HEAD] for c in range(4)], axis=1)


def kernel(
    sel_ref, len_ref, q_ref, k_ref, v_ref, w_ref,
    att_ref, out_ref,
    kv, qt, us, ms, ls, wo, ws, sib, part, relay, fin, tile_of, round_of,
    ra, rb, saz, sax, sbx, sbz, wsem, att_s, att_r, rs_s, relay_r, fin_r,
):
    seq = lax.axis_index("seq")
    head = lax.axis_index("head")
    z, x = seq // X, lax.rem(seq, X)
    y, core = head // 2, lax.rem(head, 2)

    def at(zz, xx):
        return lax.rem(zz + 2 * Z, Z) * X + lax.rem(xx + 2 * X, X)

    up, down = at(z + 1, x), at(z - 1, x)
    right, left = at(z, x + 1), at(z, x - 1)
    front = lax.rem(y + 1, Y) * 2 + core
    back = lax.rem(y + 3, Y) * 2 + core
    twin = y * 2 + 1 - core

    barrier = pltpu.get_barrier_semaphore()
    for peer in (up, down, right, left):
        pl.semaphore_signal(barrier, inc=1, device_id={"seq": peer}, device_id_type=MESH)
    for peer in (front, back, twin):
        pl.semaphore_signal(barrier, inc=1, device_id={"head": peer}, device_id_type=MESH)

    for r in range(ROUNDS):
        kv[r, seq, 0] = k_ref[r]
        for c in range(4):
            rows = slice(c * HEAD, (c + 1) * HEAD)
            kv[r, seq, 1, rows, :] = v_ref[r, rows, :].T

    pl.semaphore_wait(barrier, 7)

    def copy_a(r, block, peer, send):
        view = kv.at[r, block, :, pl.ds(0, CUT), :]
        return pltpu.make_async_remote_copy(
            src_ref=view, dst_ref=view, send_sem=send, recv_sem=ra.at[r, block],
            device_id={"seq": peer}, device_id_type=MESH,
        )

    def copy_b(r, block, peer, send):
        view = kv.at[r, block, :, pl.ds(CUT, BLOCK - CUT), :]
        return pltpu.make_async_remote_copy(
            src_ref=view, dst_ref=view, send_sem=send, recv_sem=rb.at[r, block],
            device_id={"seq": peer}, device_id_type=MESH,
        )

    def wait_a(r, block):
        copy_a(r, block, up, saz.at[r, 8]).wait_recv()

    def wait_b(r, block):
        copy_b(r, block, up, sbz.at[r, 32]).wait_recv()

    def launch(r, act):
        act(copy_b(r, seq, right, sbx.at[r, 0]))
        act(copy_b(r, seq, left, sbx.at[r, 1]))
        act(copy_a(r, seq, up, saz.at[r, z]))
        act(copy_a(r, seq, down, saz.at[r, 8]))
        act(copy_b(r, seq, up, sbz.at[r, seq]))
        act(copy_b(r, seq, down, sbz.at[r, 32 + x]))
        act(copy_a(r, seq, right, sax.at[r, z, 0]))
        act(copy_a(r, seq, left, sax.at[r, z, 1]))

    def below(r, k):
        return jnp.logical_or(
            jnp.logical_and(k == 0, r == 0), jnp.logical_and(k == Z // 2, r == 1)
        )

    def comm(r, k, i, act, waits):
        inner = jnp.logical_and(k > 0, k < Z // 2)
        lo_z, hi_z = lax.rem(z + Z - k, Z), lax.rem(z + k, Z)
        use_lo = jnp.logical_or(inner, below(r, k))
        use_hi = jnp.logical_or(inner, jnp.logical_not(below(r, k)))
        use_hi = jnp.logical_and(use_hi, jnp.logical_or(inner, jnp.logical_not(use_lo)))

        @pl.when(jnp.logical_and(i == 0, k > 0))
        def _():
            lo, hi = at(lo_z, x), at(hi_z, x)
            if waits:
                wait_a(r, lo)

            @pl.when(jnp.logical_or(k < 3, jnp.logical_and(k == 3, r == 0)))
            def _():
                act(copy_a(r, lo, up, saz.at[r, lo_z]))

            act(copy_a(r, lo, right, sax.at[r, lo_z, 0]))
            act(copy_a(r, lo, left, sax.at[r, lo_z, 1]))

            @pl.when(inner)
            def _():
                if waits:
                    wait_a(r, hi)

                @pl.when(jnp.logical_or(k < 3, r == 1))
                def _():
                    act(copy_a(r, hi, down, saz.at[r, hi_z]))

                act(copy_a(r, hi, right, sax.at[r, hi_z, 0]))
                act(copy_a(r, hi, left, sax.at[r, hi_z, 1]))

        @pl.when(i > 0)
        def _():
            off = jnp.where(i == 1, 0, jnp.where(i == 2, 1, jnp.where(i == 3, 3, 2)))
            col = lax.rem(x + off, X)
            lo, hi = at(lo_z, col), at(hi_z, col)

            @pl.when(jnp.logical_and(k == 0, i > 1))
            def _():
                if waits:
                    wait_b(r, lo)

                @pl.when(jnp.logical_and(i == 2, r == 1))
                def _():
                    act(copy_b(r, lo, left, sbx.at[r, 2]))

                @pl.when(jnp.logical_and(i == 3, r == 0))
                def _():
                    act(copy_b(r, lo, right, sbx.at[r, 2]))

                act(copy_b(r, lo, up, sbz.at[r, lo]))
                act(copy_b(r, lo, down, sbz.at[r, 32 + col]))

            @pl.when(k > 0)
            def _():
                if waits:
                    wait_b(r, lo)

                @pl.when(jnp.logical_or(k < 3, jnp.logical_and(k == 3, lax.rem(col, 2) == 0)))
                def _():
                    act(copy_b(r, lo, up, sbz.at[r, lo]))

                @pl.when(inner)
                def _():
                    if waits:
                        wait_b(r, hi)

                    @pl.when(jnp.logical_or(k < 3, lax.rem(col, 2) == 1))
                    def _():
                        act(copy_b(r, hi, down, sbz.at[r, hi]))

        @pl.when(jnp.logical_and(i == 3, use_lo))
        def _():
            block = at(lo_z, x - 1)
            if waits:
                wait_a(r, block)
            act(copy_a(r, block, right, sax.at[r, lo_z, 2]))

        @pl.when(jnp.logical_and(i == 3, use_hi))
        def _():
            block = at(hi_z, x + 1)
            if waits:
                wait_a(r, block)
            act(copy_a(r, block, left, sax.at[r, hi_z, 2]))

    def far_tile(r, block):
        query_t = qt.at[tile_of[block]]
        newer = round_of[block] == 1
        key_tile = jnp.where(newer, kv[r, block, 0], kv[0, block, 0])
        value_t = value_rows(jnp.where(newer, kv[r, block, 1], kv[0, block, 1]))
        for c in range(2):
            cols = slice(c * 256, (c + 1) * 256)
            mixed, highest, total = soft_part(key_tile, value_t, query_t[:, cols])
            us[block, :, cols] = mixed
            ms[block, :, cols] = highest
            ls[block, :, cols] = total

    def own_tile(tile, carry):
        r, h = tile // HEADS, lax.rem(tile, HEADS)
        query_t = q_ref[r, :, pl.ds(pl.multiple_of(h * HEAD, HEAD), HEAD)].T
        qt[tile] = query_t
        key_tile = kv[r, seq, 0]
        value_t = value_rows(kv[r, seq, 1])
        for c in range(2):
            cols = slice(c * 256, (c + 1) * 256)
            keys_to = (c + 1) * 256
            mixed, highest, total = soft_part(
                key_tile[:keys_to], value_t[:, :keys_to], query_t[:, cols], c * 256
            )
            us[PEERS + tile, :, cols] = mixed
            ms[PEERS + tile, :, cols] = highest
            ls[PEERS + tile, :, cols] = total
        return carry

    def compute(r, k, i):
        off = jnp.where(i == 0, 0, jnp.where(i == 1, 1, jnp.where(i == 2, 3, 2)))
        inner = jnp.logical_and(k > 0, k < Z // 2)

        def one(side, carry):
            zz = jnp.where(side == 0, z + Z - k, z + k)
            block = at(zz, x + off)
            is_below = jnp.where(inner, side == 0, below(r, k))
            live = jnp.logical_or(side == 0, inner)
            pending = jnp.logical_or(
                off == 2,
                jnp.logical_or(
                    jnp.logical_and(is_below, off == 1),
                    jnp.logical_and(jnp.logical_not(is_below), off == 3),
                ),
            )

            @pl.when(jnp.logical_and(live, pending))
            def _():
                wait_a(r, block)

            @pl.when(jnp.logical_and(live, jnp.logical_or(r == 0, block < seq)))
            def _():
                far_tile(r, block)

            return carry

        lax.fori_loop(0, 2, one, 0)

    def merge(r, h):
        tile = r * HEADS + h
        own = PEERS + tile
        slots, oks = [], []
        top = ms[own]
        for j in range(TOPK):
            chosen = sel_ref[r, 0, h, j]
            ok = chosen < r * PEERS + seq
            slot = jnp.where(ok, lax.rem(chosen, PEERS), 0)
            slots.append(slot)
            oks.append(ok)
            top = jnp.maximum(top, jnp.where(ok, ms[slot], top))
        weights = [jnp.exp2((ms[own] - top) * GAIN)]
        whole = weights[0] * ls[own]
        for slot, ok in zip(slots, oks):
            weight = jnp.where(ok, jnp.exp2(jnp.minimum(ms[slot] - top, 0.0) * GAIN), 0.0)
            weights.append(weight)
            whole = whole + weight * ls[slot]
        row = lax.broadcasted_iota(jnp.int32, (1, BLOCK), 1)
        alive = row < len_ref[0] - (r * PEERS + seq) * BLOCK
        norm = jnp.where(alive, 1.0 / whole, 0.0)
        mixed = us[own] * (weights[0] * norm)
        for slot, weight in zip(slots, weights[1:]):
            mixed = mixed + us[slot] * (weight * norm)
        rows = mixed.T.astype(jnp.bfloat16).reshape(Y, 2, 64, HEAD)
        att_ref[r, :, :, :, pl.ds(pl.multiple_of(h * HEAD, HEAD), HEAD)] = rows

    def copy_att(r):
        return pltpu.make_async_remote_copy(
            src_ref=att_ref.at[r, :, 1 - core], dst_ref=sib.at[r],
            send_sem=att_s.at[r], recv_sem=att_r.at[r],
            device_id={"head": twin}, device_id_type=MESH,
        )

    def copy_w():
        return pltpu.make_async_remote_copy(
            src_ref=w_ref, dst_ref=ws, send_sem=wsem.at[0], recv_sem=wsem.at[1],
            device_id={"head": twin}, device_id_type=MESH,
        )

    def load_w():
        return pltpu.make_async_copy(w_ref, wo, wsem.at[2])

    y_across, y_front, y_back = lax.rem(y + 2, Y), lax.rem(y + 1, Y), lax.rem(y + 3, Y)

    def copy_relay(r, n, side):
        return pltpu.make_async_remote_copy(
            src_ref=part.at[r, n, y_across, side], dst_ref=relay.at[r, n, side],
            send_sem=rs_s.at[r, n, side], recv_sem=relay_r.at[r, n, side],
            device_id={"head": front if side == 0 else back}, device_id_type=MESH,
        )

    def copy_fin(r, n, side, half):
        return pltpu.make_async_remote_copy(
            src_ref=part.at[r, n, y_front if side == 0 else y_back, half],
            dst_ref=fin.at[r, n, side, half],
            send_sem=rs_s.at[r, n, 2 + side * 2 + half], recv_sem=fin_r.at[r, n, side, half],
            device_id={"head": front if side == 0 else back}, device_id_type=MESH,
        )

    def project(r, n):
        own_rows = att_ref[r, :, core].reshape(Y * 64, HEADS * HEAD)
        twin_rows = sib[r].reshape(Y * 64, HEADS * HEAD)
        for half in range(2):
            cols = pl.ds(pl.multiple_of(n * COLS + half * HALF, HALF), HALF)
            term = jnp.dot(own_rows, wo[:, cols], preferred_element_type=jnp.float32)
            term = term + jnp.dot(twin_rows, ws[:, cols], preferred_element_type=jnp.float32)
            part[r, n, :, half] = term.astype(jnp.bfloat16).reshape(Y, 64, HALF)
        copy_relay(r, n, 0).start()
        copy_relay(r, n, 1).start()
        copy_fin(r, n, 0, 1).start()
        copy_fin(r, n, 1, 0).start()

    def pass_on(r, n):
        for side, target, half in ((0, y_front, 0), (1, y_back, 1)):
            copy_relay(r, n, side).wait_recv()
            total = part[r, n, target, half].astype(jnp.float32)
            total = total + relay[r, n, side].astype(jnp.float32)
            part[r, n, target, half] = total.astype(jnp.bfloat16)
            copy_fin(r, n, side, half).start()

    def finish(r, n):
        for side in range(2):
            for half in range(2):
                copy_fin(r, n, side, half).wait_recv()
        for half in range(2):
            total = part[r, n, y, half].astype(jnp.float32)
            total = total + fin[r, n, 0, half].astype(jnp.float32)
            total = total + fin[r, n, 1, half].astype(jnp.float32)
            cols = pl.ds(pl.multiple_of(n * COLS + half * HALF, HALF), HALF)
            out_ref[r, :, cols] = total.astype(jnp.bfloat16)

    def post(r, p):
        @pl.when(p < 4)
        def _():
            merge(r, p)

        @pl.when(p == 3)
        def _():
            copy_att(r).start()

        @pl.when(p == 4)
        def _():
            copy_att(r).wait_recv()

        @pl.when(jnp.logical_and(p == 4, r == 0))
        def _():
            load_w().wait()
            copy_w().wait_recv()

        @pl.when(jnp.logical_and(p >= 4, p < 8))
        def _():
            project(r, p - 4)

        @pl.when(jnp.logical_and(p >= 6, p < 10))
        def _():
            pass_on(r, p - 6)

        @pl.when(p >= 8)
        def _():
            finish(r, p - 8)

    def stage_of(g):
        r = jnp.where(jnp.logical_or(g == 4, g > 5), 1, 0)
        k = jnp.where(g < 4, g, jnp.where(g == 4, 0, jnp.where(g == 5, 4, g - 5)))
        return r, k

    start = lambda copy: copy.start()
    drain = lambda copy: copy.wait_send()

    launch(0, start)
    load_w().start()
    copy_w().start()

    def table(block, carry):
        tile, newer = jnp.int32(0), jnp.int32(0)
        for r in range(ROUNDS):
            for h in range(HEADS):
                for j in range(TOPK):
                    chosen = sel_ref[r, 0, h, j]
                    hit = jnp.logical_and(
                        lax.rem(chosen, PEERS) == block, chosen < r * PEERS + seq
                    )
                    tile = jnp.where(hit, r * HEADS + h, tile)
                    newer = jnp.where(hit, chosen // PEERS, newer)
        tile_of[block] = tile
        round_of[block] = newer
        return carry

    lax.fori_loop(0, ROUNDS * HEADS, own_tile, 0)
    lax.fori_loop(0, PEERS, table, 0)

    def step(t, carry):
        g, i = t // 5, lax.rem(t, 5)

        @pl.when(g < STAGES)
        def _():
            r, k = stage_of(g)
            comm(r, k, i, start, True)

        @pl.when(t == 19)
        def _():
            launch(1, start)

        @pl.when(jnp.logical_and(jnp.logical_and(g > 0, i < 4), t < COMPUTE_END))
        def _():
            r, k = stage_of(g - 1)
            compute(r, k, i)

        late = t >= POST_1
        p = t - jnp.where(late, POST_1, POST_0)

        @pl.when(jnp.logical_and(p >= 0, p < POST_STEPS))
        def _():
            post(jnp.where(late, 1, 0), p)

        return carry

    lax.fori_loop(0, POST_1 + POST_STEPS, step, 0)

    def drain_step(t, carry):
        r, k = stage_of(t // 5)
        comm(r, k, lax.rem(t, 5), drain, False)
        return carry

    launch(0, drain)
    launch(1, drain)
    lax.fori_loop(0, STAGES * 5, drain_step, 0)
    copy_w().wait_send()
    for r in range(ROUNDS):
        copy_att(r).wait_send()

        def drain_sum(n, carry, r=r):
            for side in range(2):
                copy_relay(r, n, side).wait_send()
                for half in range(2):
                    copy_fin(r, n, side, half).wait_send()
            return carry

        lax.fori_loop(0, MODEL // COLS, drain_sum, 0)


def per_device(queries, keys, values, selected, length, out_weight):
    vmem = pl.BlockSpec(memory_space=pltpu.VMEM)
    smem = pl.BlockSpec(memory_space=pltpu.SMEM)
    bf16, f32 = jnp.bfloat16, jnp.float32
    tiles = MODEL // COLS
    dma = pltpu.SemaphoreType.DMA
    attended, projected = pl.pallas_call(
        kernel,
        out_shape=(
            jax.ShapeDtypeStruct((ROUNDS, Y, 2, 64, HEADS * HEAD), bf16),
            jax.ShapeDtypeStruct((ROUNDS, 64, MODEL), bf16),
        ),
        in_specs=[smem, smem, vmem, vmem, vmem, pl.BlockSpec(memory_space=pl.ANY)],
        out_specs=(vmem, vmem),
        scratch_shapes=[
            pltpu.VMEM((ROUNDS, PEERS, 2, BLOCK, HEAD), bf16),
            pltpu.VMEM((ROUNDS * HEADS, HEAD, BLOCK), bf16),
            pltpu.VMEM((PEERS + ROUNDS * HEADS, HEAD, BLOCK), f32),
            pltpu.VMEM((PEERS + ROUNDS * HEADS, 1, BLOCK), f32),
            pltpu.VMEM((PEERS + ROUNDS * HEADS, 1, BLOCK), f32),
            pltpu.VMEM((HEADS * HEAD, MODEL), bf16),
            pltpu.VMEM((HEADS * HEAD, MODEL), bf16),
            pltpu.VMEM((ROUNDS, Y, 64, HEADS * HEAD), bf16),
            pltpu.VMEM((ROUNDS, tiles, Y, 2, 64, HALF), bf16),
            pltpu.VMEM((ROUNDS, tiles, 2, 64, HALF), bf16),
            pltpu.VMEM((ROUNDS, tiles, 2, 2, 64, HALF), bf16),
            pltpu.SMEM((PEERS,), jnp.int32),
            pltpu.SMEM((PEERS,), jnp.int32),
            dma((ROUNDS, PEERS)),
            dma((ROUNDS, PEERS)),
            dma((ROUNDS, Z + 1)),
            dma((ROUNDS, Z, 3)),
            dma((ROUNDS, 3)),
            dma((ROUNDS, PEERS + X)),
            dma((3,)),
            dma((ROUNDS,)),
            dma((ROUNDS,)),
            dma((ROUNDS, tiles, 6)),
            dma((ROUNDS, tiles, 2)),
            dma((ROUNDS, tiles, 2, 2)),
        ],
        compiler_params=pltpu.CompilerParams(
            collective_id=0, has_side_effects=True, vmem_limit_bytes=60 * 1024 * 1024
        ),
        cost_estimate=pl.CostEstimate(
            flops=72 * 4 * BLOCK * BLOCK * HEAD, bytes_accessed=8 * 1024 * 1024, transcendentals=72 * BLOCK * BLOCK
        ),
        name="attend_and_project",
    )(selected, length, queries, keys, values, out_weight)
    return attended.reshape(ROUNDS, BLOCK, HEADS * HEAD), projected


def solution(mesh):
    placed = (
        P(None, "seq", "head"),
        P(None, "seq", "head"),
        P(None, "seq", "head"),
        P(None, "seq", "head", None),
        P(),
        P("head", None),
    )
    return jax.shard_map(
        per_device,
        mesh=mesh,
        in_specs=placed,
        out_specs=(P(None, "seq", "head"), P(None, ("seq", "head"), None)),
        check_vma=False,
    )
```

time: 324 us -> 160 us (0.49)
  waiting for transfers between devices: 262 us -> 0 us
  Pallas kernels: 16.3 us -> 149 us
  between operations: 14.5 us -> 1.29 us
  other arithmetic: 12.8 us -> 0 us
  matrix products: 8.73 us -> 0 us
    all_gather x2 -> x0, waiting for transfers between devices: 199 us -> none  [per_device(): lax.all_gather(jnp.stack([keys[r], values[r]]), 'seq', axis=0)]
    pallas_call x2 -> x1, Pallas kernels: 16.3 us -> 149 us  [per_device(): pl.pallas_call(kernel, out_shape=(jax.ShapeDtypeStruct((ROUNDS, Y, 2, 64,...]
    reduce_scatter x2 -> x0, waiting for transfers between devices: 63.7 us -> none  [per_device(): lax.psum_scatter(term, 'head', scatter_dimension=0, tiled=True)]
    dot_general x2 -> x0, matrix products: 8.73 us -> none  [per_device(): jnp.dot(rows, out_weight, preferred_element_type=jnp.float32)]
    concatenate x1 -> x0, other arithmetic: 7.97 us -> none  [per_device(): far = gathered[0] if r == 0 else jnp.concatenate(gathered[:r + 1], axis=1)]
    another operation x4 -> x0, other arithmetic: 4.78 us -> none  [the longest x2 3.33 us: per_device(): return (jnp.stack(attended), jnp.stack(projected))]
  transfers between devices with their start and end apart: 4 -> 0, of which waited for: 4 -> 0; matrix products, arithmetic and copies ran while one was open for 3% -> 0% of each run, Pallas kernels for 1% -> 0%
where the time goes in v2:
time: 160 us; the launch traced here: 156 us
  Pallas kernels  149 us (93%)
  local copies, waits for them, and re-layouts  5.91 us (4%)
    pallas_call x1, Pallas kernels, per_device(): pl.pallas_call(kernel, out_shape=(jax.ShapeDtypeStruct((ROUNDS, Y, 2, 64,...  149 us
    unnamed x3, local copies, waits for them, and re-layouts  5.91 us

profile of v2, /device:TPU:1, one launch (start us, length us, event | category | flops | bytes accessed | tf_op | source)
XLA Modules:
  0.0 156.5 jit_solution(13477358263092087748)
XLA Ops:
  1.3 1.4 copy.8.sel_ref
  2.6 149.3 %attend_and_project.1 = (bf16[2,4,2,64,512]{4,3,2,1,0:T(8,128)(2,1)}, bf16[2,64,4096]{2,1,0:T(8,128)(2,1)}) custom-call(s32[2,1,4,3]{3,2,1,0:T(4,128)} %copy.8.sel_ref, s32[1]{0:T(128)S(6)} %copy.11.len_ref, bf16[2,512,512]{2,1,0:T(8,128)(2,1)} %q_ref.1, bf16[2,512,128]{2,1,0:T(8,128)(2,1)} %k_ref.1, bf16[2,512,128]{2,1,0:T(8,128)(2,1)} %v_ref.1, ...), custom_call_target="tpu_custom_call" | custom-call | flops 9663676416 | bytes 8388608 | tf_op jit(solution)/shard_map/attend_and_project/pallas_call | solution.py:466
  151.9 2.3 %copy.12 = bf16[2,512,512]{2,1,0:T(8,128)(2,1)} copy(bf16[2,512,512]{2,1,0:T(8,128)(2,1)} %bitcast.1) | data formatting | bytes 2097152
  154.2 2.3 %copy.13 = bf16[2,64,4096]{2,1,0:T(8,128)(2,1)} copy(bf16[2,64,4096]{2,1,0:T(8,128)(2,1)} %get-tuple-element.9) | data formatting | bytes 2097152

commit v3 on v2

v3 whole, which is shorter than its diff:
```python
import jax
import jax.numpy as jnp
from jax import lax
from jax.experimental import pallas as pl
from jax.experimental.pallas import tpu as pltpu
from jax.sharding import PartitionSpec as P

HEAD = 128
Z, X, Y = 8, 4, 4
PEERS = Z * X
BLOCK = 512
HEADS = 4
TOPK = 3
ROUNDS = 2
MODEL = 4096
GAIN = HEAD ** (-0.5) * 1.4426950408889634
CUT = 304
COLS = 1024
HALF = COLS // 2
TILES = MODEL // COLS
MESH = pl.DeviceIdType.MESH
STEPS = 102
FORWARD = (
    5179011, 524288, 17, 67895296, 206483, 4718627, 33, 109922067,
    12862515, 149171, 17065395, 3245635, 3565507, 66, 84677657, 7149451,
    0, 107762176, 79360, 14955563, 218891, 44826624, 19166720, 116274730,
    95744, 19437056, 120354091, 161483, 331, 0, 0, 0,
    0, 0,
)
WORK = (
    4718592, 1025, 13173257, 4474241, 67384320, 29738, 38216225, 139776,
    12927488, 109462016, 46399498, 17039793, 0, 117801777, 0, 103092736,
    5145113, 9175043, 5244979, 13631524, 69478917, 107235993, 1600041, 5984937,
    14969894, 37657, 115700224, 52843465, 3044169, 15488539, 11548684, 7632909,
    16013838, 16276510,
)


def soft_part(key_tile, value_t, query_t, mask_from=None):
    scores = jnp.dot(key_tile, query_t, preferred_element_type=jnp.float32)
    if mask_from is not None:
        key_at = lax.broadcasted_iota(jnp.int32, scores.shape, 0)
        query_at = lax.broadcasted_iota(jnp.int32, scores.shape, 1) + mask_from
        scores = jnp.where(key_at <= query_at, scores, -1e30)
    highest = jnp.max(scores, axis=0, keepdims=True)
    weights = jnp.exp2((scores - highest) * GAIN)
    total = jnp.sum(weights, axis=0, keepdims=True)
    mixed = jnp.dot(value_t, weights.astype(jnp.bfloat16), preferred_element_type=jnp.float32)
    return mixed, highest, total


def value_rows(stacked):
    return jnp.concatenate([stacked[c * HEAD : (c + 1) * HEAD] for c in range(4)], axis=1)


def kernel(
    sel_ref, len_ref, q_ref, k_ref, v_ref, w_ref,
    att_ref, out_ref,
    kv, qv, vv, qt, us, ms, ls, wo, ws, attx, sib, part, relay, fin, outv, tile_of, round_of,
    ra, rb, saz, sax, sbx, sbz, insem, wsem, att_s, att_r, rs_s, relay_r, fin_r, att_o, out_o,
):
    seq = lax.axis_index("seq")
    head = lax.axis_index("head")
    z, x = seq // X, lax.rem(seq, X)
    y, core = head // 2, lax.rem(head, 2)

    def at(zz, xx):
        return lax.rem(zz + 2 * Z, Z) * X + lax.rem(xx + 2 * X, X)

    up, down = at(z + 1, x), at(z - 1, x)
    right, left = at(z, x + 1), at(z, x - 1)
    front = lax.rem(y + 1, Y) * 2 + core
    back = lax.rem(y + 3, Y) * 2 + core
    twin = y * 2 + 1 - core

    barrier = pltpu.get_barrier_semaphore()
    for peer in (up, down, right, left):
        pl.semaphore_signal(barrier, inc=1, device_id={"seq": peer}, device_id_type=MESH)
    for peer in (front, back, twin):
        pl.semaphore_signal(barrier, inc=1, device_id={"head": peer}, device_id_type=MESH)

    load_v = pltpu.make_async_copy(v_ref, vv, insem.at[0])
    load_k = [
        pltpu.make_async_copy(k_ref.at[r], kv.at[r, seq, 0], insem.at[1 + r]) for r in range(ROUNDS)
    ]
    load_q = pltpu.make_async_copy(q_ref, qv, insem.at[3])
    load_w = pltpu.make_async_copy(w_ref, wo, wsem.at[2])
    load_v.start()
    for load in load_k:
        load.start()
    load_q.start()
    load_v.wait()
    for r in range(ROUNDS):
        for c in range(4):
            rows = slice(c * HEAD, (c + 1) * HEAD)
            kv[r, seq, 1, rows, :] = vv[r, rows, :].T
    for load in load_k:
        load.wait()
    pl.semaphore_wait(barrier, 7)

    def copy_a(r, block, peer, send):
        view = kv.at[r, block, :, pl.ds(0, CUT), :]
        return pltpu.make_async_remote_copy(
            src_ref=view, dst_ref=view, send_sem=send, recv_sem=ra.at[r, block],
            device_id={"seq": peer}, device_id_type=MESH,
        )

    def copy_b(r, block, peer, send):
        view = kv.at[r, block, :, pl.ds(CUT, BLOCK - CUT), :]
        return pltpu.make_async_remote_copy(
            src_ref=view, dst_ref=view, send_sem=send, recv_sem=rb.at[r, block],
            device_id={"seq": peer}, device_id_type=MESH,
        )

    def wait_a(r, block):
        copy_a(r, block, up, saz.at[r, 8]).wait_recv()

    def wait_b(r, block):
        copy_b(r, block, up, sbz.at[r, 32]).wait_recv()

    def launch_b(r, act):
        act(copy_b(r, seq, right, sbx.at[r, 0]))
        act(copy_b(r, seq, left, sbx.at[r, 1]))
        act(copy_b(r, seq, up, sbz.at[r, seq]))
        act(copy_b(r, seq, down, sbz.at[r, 32 + x]))

    def launch_a(r, act):
        act(copy_a(r, seq, up, saz.at[r, z]))
        act(copy_a(r, seq, down, saz.at[r, 8]))
        act(copy_a(r, seq, right, sax.at[r, z, 0]))
        act(copy_a(r, seq, left, sax.at[r, z, 1]))

    def inner_of(k):
        return jnp.logical_and(k > 0, k < Z // 2)

    def below(r, k):
        return jnp.logical_or(
            jnp.logical_and(k == 0, r == 0), jnp.logical_and(k == Z // 2, r == 1)
        )

    def forward_a(r, k, act, waits):
        lo_z, hi_z = lax.rem(z + Z - k, Z), lax.rem(z + k, Z)
        lo, hi = at(lo_z, x), at(hi_z, x)
        if waits:
            wait_a(r, lo)

        @pl.when(jnp.logical_or(k < 3, jnp.logical_and(k == 3, r == 0)))
        def _():
            act(copy_a(r, lo, up, saz.at[r, lo_z]))

        act(copy_a(r, lo, right, sax.at[r, lo_z, 0]))
        act(copy_a(r, lo, left, sax.at[r, lo_z, 1]))

        @pl.when(k < 4)
        def _():
            if waits:
                wait_a(r, hi)

            @pl.when(jnp.logical_or(k < 3, r == 1))
            def _():
                act(copy_a(r, hi, down, saz.at[r, hi_z]))

            act(copy_a(r, hi, right, sax.at[r, hi_z, 0]))
            act(copy_a(r, hi, left, sax.at[r, hi_z, 1]))

    def forward_f(r, k, act, waits):
        lo_z, hi_z = lax.rem(z + Z - k, Z), lax.rem(z + k, Z)
        inner, is_below = inner_of(k), below(r, k)

        @pl.when(jnp.logical_or(inner, is_below))
        def _():
            block = at(lo_z, x - 1)
            if waits:
                wait_a(r, block)
            act(copy_a(r, block, right, sax.at[r, lo_z, 2]))

        @pl.when(jnp.logical_or(inner, jnp.logical_not(is_below)))
        def _():
            block = at(hi_z, x + 1)
            if waits:
                wait_a(r, block)
            act(copy_a(r, block, left, sax.at[r, hi_z, 2]))

    def forward_b(r, k, off, act, waits):
        lo_z, hi_z = lax.rem(z + Z - k, Z), lax.rem(z + k, Z)
        col = lax.rem(x + off, X)
        lo, hi = at(lo_z, col), at(hi_z, col)
        if waits:
            wait_b(r, lo)

        @pl.when(k == 0)
        def _():
            @pl.when(jnp.logical_and(off == 1, r == 1))
            def _():
                act(copy_b(r, lo, left, sbx.at[r, 2]))

            @pl.when(jnp.logical_and(off == 3, r == 0))
            def _():
                act(copy_b(r, lo, right, sbx.at[r, 2]))

            act(copy_b(r, lo, up, sbz.at[r, lo]))
            act(copy_b(r, lo, down, sbz.at[r, 32 + col]))

        @pl.when(k > 0)
        def _():
            @pl.when(jnp.logical_or(k < 3, jnp.logical_and(k == 3, lax.rem(col, 2) == 0)))
            def _():
                act(copy_b(r, lo, up, sbz.at[r, lo]))

            @pl.when(k < 4)
            def _():
                if waits:
                    wait_b(r, hi)

                @pl.when(jnp.logical_or(k < 3, lax.rem(col, 2) == 1))
                def _():
                    act(copy_b(r, hi, down, sbz.at[r, hi]))

    def far_tile(r, block):
        query_t = qt.at[tile_of[block]]
        newer = round_of[block] == 1
        key_tile = jnp.where(newer, kv[r, block, 0], kv[0, block, 0])
        value_t = value_rows(jnp.where(newer, kv[r, block, 1], kv[0, block, 1]))
        for c in range(2):
            cols = slice(c * 256, (c + 1) * 256)
            mixed, highest, total = soft_part(key_tile, value_t, query_t[:, cols])
            us[block, :, cols] = mixed
            ms[block, :, cols] = highest
            ls[block, :, cols] = total

    def own_tile(r, h):
        tile = r * HEADS + h
        key_tile = kv[r, seq, 0]
        value_t = value_rows(kv[r, seq, 1])
        for c in range(2):
            cols = slice(c * 256, (c + 1) * 256)
            keys_to = (c + 1) * 256
            mixed, highest, total = soft_part(
                key_tile[:keys_to], value_t[:, :keys_to], qt[tile, :, cols], c * 256
            )
            us[PEERS + tile, :, cols] = mixed
            ms[PEERS + tile, :, cols] = highest
            ls[PEERS + tile, :, cols] = total

    def far_slots(r, k, off):
        inner, is_below = inner_of(k), below(r, k)

        def one(side, carry):
            zz = jnp.where(side == 0, z + Z - k, z + k)
            block = at(zz, x + off)
            from_left = jnp.where(inner, side == 0, is_below)
            live = jnp.logical_or(side == 0, inner)
            pending = jnp.logical_or(
                off == 2,
                jnp.logical_or(
                    jnp.logical_and(from_left, off == 1),
                    jnp.logical_and(jnp.logical_not(from_left), off == 3),
                ),
            )

            @pl.when(jnp.logical_and(live, pending))
            def _():
                wait_a(r, block)

            @pl.when(jnp.logical_and(live, jnp.logical_or(r == 0, block < seq)))
            def _():
                far_tile(r, block)

            return carry

        lax.fori_loop(0, 2, one, 0)

    def copy_att(r, h):
        return pltpu.make_async_remote_copy(
            src_ref=attx.at[r, 1 - core, h], dst_ref=sib.at[r, h],
            send_sem=att_s.at[r, h], recv_sem=att_r.at[r, h],
            device_id={"head": twin}, device_id_type=MESH,
        )

    def store_att(r, h, c):
        cols = pl.ds(pl.multiple_of(h * HEAD, HEAD), HEAD)
        return pltpu.make_async_copy(
            attx.at[r, c, h], att_ref.at[r, :, c, :, cols], att_o.at[r, h, c]
        )

    def merge(r, h):
        tile = r * HEADS + h
        own = PEERS + tile
        slots, oks = [], []
        top = ms[own]
        for j in range(TOPK):
            chosen = sel_ref[r, j, 0, h]
            ok = chosen < r * PEERS + seq
            slot = jnp.where(ok, lax.rem(chosen, PEERS), 0)
            slots.append(slot)
            oks.append(ok)
            top = jnp.maximum(top, jnp.where(ok, ms[slot], top))
        weights = [jnp.exp2((ms[own] - top) * GAIN)]
        whole = weights[0] * ls[own]
        for slot, ok in zip(slots, oks):
            weight = jnp.where(ok, jnp.exp2(jnp.minimum(ms[slot] - top, 0.0) * GAIN), 0.0)
            weights.append(weight)
            whole = whole + weight * ls[slot]
        row = lax.broadcasted_iota(jnp.int32, (1, BLOCK), 1)
        alive = row < len_ref[0] - (r * PEERS + seq) * BLOCK
        norm = jnp.where(alive, 1.0 / whole, 0.0)
        mixed = us[own] * (weights[0] * norm)
        for slot, weight in zip(slots, weights[1:]):
            mixed = mixed + us[slot] * (weight * norm)
        rows = mixed.T.astype(jnp.bfloat16).reshape(Y, 2, 64, HEAD)
        for c in range(2):
            attx[r, c, h] = rows[:, c]
        copy_att(r, h).start()
        for c in range(2):
            store_att(r, h, c).start()

    def copy_w():
        return pltpu.make_async_remote_copy(
            src_ref=w_ref, dst_ref=ws, send_sem=wsem.at[0], recv_sem=wsem.at[1],
            device_id={"head": twin}, device_id_type=MESH,
        )

    y_across, y_front, y_back = lax.rem(y + 2, Y), lax.rem(y + 1, Y), lax.rem(y + 3, Y)

    def copy_relay(r, n, side):
        return pltpu.make_async_remote_copy(
            src_ref=part.at[r, n, y_across, side], dst_ref=relay.at[r, n, side],
            send_sem=rs_s.at[r, n, side], recv_sem=relay_r.at[r, n, side],
            device_id={"head": front if side == 0 else back}, device_id_type=MESH,
        )

    def copy_fin(r, n, side, half):
        return pltpu.make_async_remote_copy(
            src_ref=part.at[r, n, y_front if side == 0 else y_back, half],
            dst_ref=fin.at[r, n, side, half],
            send_sem=rs_s.at[r, n, 2 + side * 2 + half], recv_sem=fin_r.at[r, n, side, half],
            device_id={"head": front if side == 0 else back}, device_id_type=MESH,
        )

    def project(r, n):
        own_rows = jnp.concatenate(
            [attx[r, core, h].reshape(Y * 64, HEAD) for h in range(HEADS)], axis=1
        )
        twin_rows = jnp.concatenate(
            [sib[r, h].reshape(Y * 64, HEAD) for h in range(HEADS)], axis=1
        )
        for half in range(2):
            cols = pl.ds(pl.multiple_of(n * COLS + half * HALF, HALF), HALF)
            term = jnp.dot(own_rows, wo[:, cols], preferred_element_type=jnp.float32)
            term = term + jnp.dot(twin_rows, ws[:, cols], preferred_element_type=jnp.float32)
            part[r, n, :, half] = term.astype(jnp.bfloat16).reshape(Y, 64, HALF)
        copy_relay(r, n, 0).start()
        copy_relay(r, n, 1).start()
        copy_fin(r, n, 0, 1).start()
        copy_fin(r, n, 1, 0).start()

    def pass_on(r, n):
        for side, target, half in ((0, y_front, 0), (1, y_back, 1)):
            copy_relay(r, n, side).wait_recv()
            total = part[r, n, target, half].astype(jnp.float32)
            total = total + relay[r, n, side].astype(jnp.float32)
            part[r, n, target, half] = total.astype(jnp.bfloat16)
            copy_fin(r, n, side, half).start()

    def store_out(r, n):
        cols = pl.ds(pl.multiple_of(n * COLS, COLS), COLS)
        return pltpu.make_async_copy(outv.at[r, :, cols], out_ref.at[r, :, cols], out_o.at[r, n])

    def finish(r, n):
        for side in range(2):
            for half in range(2):
                copy_fin(r, n, side, half).wait_recv()
        for half in range(2):
            total = part[r, n, y, half].astype(jnp.float32)
            total = total + fin[r, n, 0, half].astype(jnp.float32)
            total = total + fin[r, n, 1, half].astype(jnp.float32)
            cols = pl.ds(pl.multiple_of(n * COLS + half * HALF, HALF), HALF)
            outv[r, :, cols] = total.astype(jnp.bfloat16)
        store_out(r, n).start()

    start = lambda copy: copy.start()
    drain = lambda copy: copy.wait_send()

    launch_b(0, start)
    launch_a(0, start)
    copy_w().start()
    load_w.start()

    def table(block, carry):
        tile, newer = jnp.int32(0), jnp.int32(0)
        for r in range(ROUNDS):
            for h in range(HEADS):
                for j in range(TOPK):
                    chosen = sel_ref[r, j, 0, h]
                    hit = jnp.logical_and(
                        lax.rem(chosen, PEERS) == block, chosen < r * PEERS + seq
                    )
                    tile = jnp.where(hit, r * HEADS + h, tile)
                    newer = jnp.where(hit, chosen // PEERS, newer)
        tile_of[block] = tile
        round_of[block] = newer
        return carry

    load_q.wait()
    for r in range(ROUNDS):
        for h in range(HEADS):
            qt[r * HEADS + h] = qv[r, :, h * HEAD : (h + 1) * HEAD].T
    lax.fori_loop(0, PEERS, table, 0)

    def step(t, carry):
        forward, work_code = jnp.int32(FORWARD[0]), jnp.int32(WORK[0])
        third = t // 3
        for w in range(1, len(FORWARD)):
            here = third == w
            forward = jnp.where(here, FORWARD[w], forward)
            work_code = jnp.where(here, WORK[w], work_code)
        bits = lax.rem(t, 3) * 9
        forward, work_code = forward >> bits, work_code >> bits
        kind, r, k, off = forward & 7, (forward >> 3) & 1, (forward >> 4) & 7, (forward >> 7) & 3

        @pl.when(kind == 1)
        def _():
            forward_a(r, k, start, True)

        @pl.when(kind == 2)
        def _():
            forward_f(r, k, start, True)

        @pl.when(kind == 3)
        def _():
            forward_b(r, k, off, start, True)

        @pl.when(kind == 4)
        def _():
            launch_a(1, start)

        @pl.when(kind == 5)
        def _():
            launch_b(1, start)

        work, wr = work_code & 7, (work_code >> 3) & 1
        item, woff = (work_code >> 4) & 7, (work_code >> 7) & 3

        @pl.when(work == 1)
        def _():
            far_slots(wr, item, woff)

        @pl.when(work == 2)
        def _():
            own_tile(wr, item)

        @pl.when(work == 3)
        def _():
            merge(wr, item)

        @pl.when(work == 4)
        def _():
            @pl.when(item == 0)
            def _():
                @pl.when(wr == 0)
                def _():
                    load_w.wait()
                    copy_w().wait_recv()

                for h in range(HEADS):
                    copy_att(wr, h).wait_recv()

            project(wr, item)

        @pl.when(work == 5)
        def _():
            pass_on(wr, item)

        @pl.when(work == 6)
        def _():
            finish(wr, item)

        return carry

    lax.fori_loop(0, STEPS, step, 0)

    def drain_step(t, carry):
        r, k, off = t // 20, lax.rem(t // 4, 5), lax.rem(t, 4)

        @pl.when(jnp.logical_or(k > 0, off > 0))
        def _():
            forward_b(r, k, off, drain, False)

        @pl.when(off == 0)
        def _():
            forward_f(r, k, drain, False)

        @pl.when(jnp.logical_and(off == 0, k > 0))
        def _():
            forward_a(r, k, drain, False)

        return carry

    for r in range(ROUNDS):
        launch_a(r, drain)
        launch_b(r, drain)
    lax.fori_loop(0, ROUNDS * 20, drain_step, 0)
    copy_w().wait_send()

    def drain_sum(t, carry):
        r, n = t // TILES, lax.rem(t, TILES)
        copy_att(r, n).wait_send()
        for c in range(2):
            store_att(r, n, c).wait()
        for side in range(2):
            copy_relay(r, n, side).wait_send()
            for half in range(2):
                copy_fin(r, n, side, half).wait_send()
        store_out(r, n).wait()
        return carry

    lax.fori_loop(0, ROUNDS * TILES, drain_sum, 0)


def hand_over(att_in, out_in, att_ref, out_ref, sems):
    copies = []
    for r in range(ROUNDS):
        for i in range(2):
            rows = slice(i * 256, (i + 1) * 256)
            copies.append((att_in.at[r, rows, :], att_ref.at[r, rows, :]))
            rows = slice(i * 32, (i + 1) * 32)
            copies.append((out_in.at[r, rows, :], out_ref.at[r, rows, :]))
    copies = [pltpu.make_async_copy(a, b, sems.at[i]) for i, (a, b) in enumerate(copies)]
    for copy in copies:
        copy.start()
    for copy in copies:
        copy.wait()


def per_device(queries, keys, values, selected, length, out_weight):
    anywhere = pl.BlockSpec(memory_space=pl.ANY)
    smem = pl.BlockSpec(memory_space=pltpu.SMEM)
    bf16, f32 = jnp.bfloat16, jnp.float32
    dma = pltpu.SemaphoreType.DMA
    attended, projected = pl.pallas_call(
        kernel,
        out_shape=(
            jax.ShapeDtypeStruct((ROUNDS, Y, 2, 64, HEADS * HEAD), bf16),
            jax.ShapeDtypeStruct((ROUNDS, 64, MODEL), bf16),
        ),
        in_specs=[smem, smem, anywhere, anywhere, anywhere, anywhere],
        out_specs=(anywhere, anywhere),
        scratch_shapes=[
            pltpu.VMEM((ROUNDS, PEERS, 2, BLOCK, HEAD), bf16),
            pltpu.VMEM((ROUNDS, BLOCK, HEADS * HEAD), bf16),
            pltpu.VMEM((ROUNDS, BLOCK, HEAD), bf16),
            pltpu.VMEM((ROUNDS * HEADS, HEAD, BLOCK), bf16),
            pltpu.VMEM((PEERS + ROUNDS * HEADS, HEAD, BLOCK), f32),
            pltpu.VMEM((PEERS + ROUNDS * HEADS, 1, BLOCK), f32),
            pltpu.VMEM((PEERS + ROUNDS * HEADS, 1, BLOCK), f32),
            pltpu.VMEM((HEADS * HEAD, MODEL), bf16),
            pltpu.VMEM((HEADS * HEAD, MODEL), bf16),
            pltpu.VMEM((ROUNDS, 2, HEADS, Y, 64, HEAD), bf16),
            pltpu.VMEM((ROUNDS, HEADS, Y, 64, HEAD), bf16),
            pltpu.VMEM((ROUNDS, TILES, Y, 2, 64, HALF), bf16),
            pltpu.VMEM((ROUNDS, TILES, 2, 64, HALF), bf16),
            pltpu.VMEM((ROUNDS, TILES, 2, 2, 64, HALF), bf16),
            pltpu.VMEM((ROUNDS, 64, MODEL), bf16),
            pltpu.SMEM((PEERS,), jnp.int32),
            pltpu.SMEM((PEERS,), jnp.int32),
            dma((ROUNDS, PEERS)),
            dma((ROUNDS, PEERS)),
            dma((ROUNDS, Z + 1)),
            dma((ROUNDS, Z, 3)),
            dma((ROUNDS, 3)),
            dma((ROUNDS, PEERS + X)),
            dma((4,)),
            dma((3,)),
            dma((ROUNDS, HEADS)),
            dma((ROUNDS, HEADS)),
            dma((ROUNDS, TILES, 6)),
            dma((ROUNDS, TILES, 2)),
            dma((ROUNDS, TILES, 2, 2)),
            dma((ROUNDS, HEADS, 2)),
            dma((ROUNDS, TILES)),
        ],
        compiler_params=pltpu.CompilerParams(
            collective_id=0, has_side_effects=True, vmem_limit_bytes=60 * 1024 * 1024
        ),
        cost_estimate=pl.CostEstimate(
            flops=72 * 4 * BLOCK * BLOCK * HEAD,
            bytes_accessed=8 * 1024 * 1024,
            transcendentals=72 * BLOCK * BLOCK,
        ),
        name="attend_and_project",
    )(selected.transpose(0, 3, 1, 2), length, queries, keys, values, out_weight)
    attended = attended.reshape(ROUNDS, BLOCK, HEADS * HEAD)
    return pl.pallas_call(
        hand_over,
        out_shape=(
            jax.ShapeDtypeStruct(attended.shape, bf16),
            jax.ShapeDtypeStruct(projected.shape, bf16),
        ),
        in_specs=[anywhere, anywhere],
        out_specs=(anywhere, anywhere),
        scratch_shapes=[dma((8,))],
        name="hand_over",
    )(attended, projected)


def solution(mesh):
    placed = (
        P(None, "seq", "head"),
        P(None, "seq", "head"),
        P(None, "seq", "head"),
        P(None, "seq", "head", None),
        P(),
        P("head", None),
    )
    return jax.shard_map(
        per_device,
        mesh=mesh,
        in_specs=placed,
        out_specs=(P(None, "seq", "head"), P(None, ("seq", "head"), None)),
        check_vma=False,
    )
```

time: 160 us -> 209 us (1.31); the launches traced: 156 us -> 209 us
  Pallas kernels: 149 us -> 208 us
  local copies, waits for them, and re-layouts: 5.91 us -> 0 us
    pallas_call x0 -> x1, Pallas kernels: none -> 64.7 us  [per_device(): pl.pallas_call(hand_over, out_shape=(jax.ShapeDtypeStruct(attended.shape,...]
    pallas_call x1, Pallas kernels: 149 us -> 143 us  [per_device(): pl.pallas_call(kernel, out_shape=(jax.ShapeDtypeStruct((ROUNDS, Y, 2, 64,...]
    unnamed x3 -> x0, local copies, waits for them, and re-layouts: 5.91 us -> none
where the time goes in v3:
time: 209 us
  Pallas kernels  208 us (100%)
    pallas_call x1, Pallas kernels, per_device(): pl.pallas_call(kernel, out_shape=(jax.ShapeDtypeStruct((ROUNDS, Y, 2, 64,...  143 us
    pallas_call x1, Pallas kernels, per_device(): pl.pallas_call(hand_over, out_shape=(jax.ShapeDtypeStruct(attended.shape,...  64.7 us

profile of v3, /device:TPU:1, one launch (start us, length us, event | category | flops | bytes accessed | tf_op | source)
XLA Modules:
  0.0 209.1 jit_solution(6284098961498297326)
XLA Ops:
  1.3 143.1 %attend_and_project.1 = (bf16[2,4,2,64,512]{4,3,2,1,0:T(8,128)(2,1)}, bf16[2,64,4096]{2,1,0:T(8,128)(2,1)}) custom-call(s32[2,3,1,4]{3,2,1,0:T(1,128)} %bitcast.3, s32[1]{0:T(128)S(6)} %copy.8.len_ref, bf16[2,512,512]{2,1,0:T(8,128)(2,1)} %q_ref.1, bf16[2,512,128]{2,1,0:T(8,128)(2,1)} %k_ref.1, bf16[2,512,128]{2,1,0:T(8,128)(2,1)} %v_ref.1, ...), custom_call_target="tpu_custom_call" | custom-call | flops 9663676416 | bytes 8388608 | tf_op jit(solution)/shard_map/attend_and_project/pallas_call | solution.py:540
  144.4 64.7 %hand_over.1 = (bf16[2,512,512]{2,1,0:T(8,128)(2,1)}, bf16[2,64,4096]{2,1,0:T(8,128)(2,1)}) custom-call(bf16[2,512,512]{2,1,0:T(8,128)(2,1)} %bitcast.2, bf16[2,64,4096]{2,1,0:T(8,128)(2,1)} %get-tuple-element.5.out_in), custom_call_target="tpu_custom_call" | custom-call | tf_op jit(solution)/shard_map/hand_over/pallas_call | solution.py:593

commit v4 on v3

--- a/solution.py
+++ b/solution.py
@@ -19,20 +19,20 @@
 HALF = COLS // 2
 TILES = MODEL // COLS
 MESH = pl.DeviceIdType.MESH
-STEPS = 102
+STEPS = 104
 FORWARD = (
-    5179011, 524288, 17, 67895296, 206483, 4718627, 33, 109922067,
-    12862515, 149171, 17065395, 3245635, 3565507, 66, 84677657, 7149451,
-    0, 107762176, 79360, 14955563, 218891, 44826624, 19166720, 116274730,
-    95744, 19437056, 120354091, 161483, 331, 0, 0, 0,
-    0, 0,
+    4989827, 8718083, 0, 9381394, 8914067, 49, 42729747, 26531,
+    3294785, 91661, 114066482, 17720832, 103546905, 36438016, 118248259, 99867,
+    70202880, 79386, 57, 74405419, 87562, 15488073, 15431168, 0,
+    78418944, 19895995, 53376512, 169472, 0, 0, 0, 0,
+    0, 0, 0,
 )
 WORK = (
-    4718592, 1025, 13173257, 4474241, 67384320, 29738, 38216225, 139776,
-    12927488, 109462016, 46399498, 17039793, 0, 117801777, 0, 103092736,
-    5145113, 9175043, 5244979, 13631524, 69478917, 107235993, 1600041, 5984937,
-    14969894, 37657, 115700224, 52843465, 3044169, 15488539, 11548684, 7632909,
-    16013838, 16276510,
+    0, 6815744, 15229962, 0, 8650752, 105129345, 17425, 42206208,
+    33816625, 67584512, 71565601, 17039505, 11231745, 103178929, 9, 84247489,
+    17923, 6563379, 5245337, 9437184, 73689088, 5722624, 10834569, 115634953,
+    40110645, 119799993, 52843081, 3052345, 7099963, 7346213, 7632940, 3435565,
+    9972742, 12074045, 31758,
 )
 
 
@@ -517,19 +517,29 @@
     lax.fori_loop(0, ROUNDS * TILES, drain_sum, 0)
 
 
-def hand_over(att_in, out_in, att_ref, out_ref, sems):
-    copies = []
+def hand_over(att_in, out_in, att_ref, out_ref, att_v, out_v, sems):
+    places = []
     for r in range(ROUNDS):
         for i in range(2):
             rows = slice(i * 256, (i + 1) * 256)
-            copies.append((att_in.at[r, rows, :], att_ref.at[r, rows, :]))
+            places.append((att_in, att_v, att_ref, r, rows))
             rows = slice(i * 32, (i + 1) * 32)
-            copies.append((out_in.at[r, rows, :], out_ref.at[r, rows, :]))
-    copies = [pltpu.make_async_copy(a, b, sems.at[i]) for i, (a, b) in enumerate(copies)]
-    for copy in copies:
-        copy.start()
-    for copy in copies:
-        copy.wait()
+            places.append((out_in, out_v, out_ref, r, rows))
+    loads, stores = [], []
+    for i, (src, mid, dst, r, rows) in enumerate(places):
+        loads.append(
+            pltpu.make_async_copy(src.at[r, rows, :], mid.at[r, rows, :], sems.at[0, i])
+        )
+        stores.append(
+            pltpu.make_async_copy(mid.at[r, rows, :], dst.at[r, rows, :], sems.at[1, i])
+        )
+    for load in loads:
+        load.start()
+    for load, store in zip(loads, stores):
+        load.wait()
+        store.start()
+    for store in stores:
+        store.wait()
 
 
 def per_device(queries, keys, values, selected, length, out_weight):
@@ -598,7 +608,12 @@
         ),
         in_specs=[anywhere, anywhere],
         out_specs=(anywhere, anywhere),
-        scratch_shapes=[dma((8,))],
+        scratch_shapes=[
+            pltpu.VMEM(attended.shape, bf16),
+            pltpu.VMEM(projected.shape, bf16),
+            dma((2, 8)),
+        ],
+        compiler_params=pltpu.CompilerParams(vmem_limit_bytes=60 * 1024 * 1024),
         name="hand_over",
     )(attended, projected)
 

time: 209 us -> 148 us (0.71)
  Pallas kernels: 208 us -> 147 us
    pallas_call x1, Pallas kernels: 64.7 us -> 2.4 us  [per_device(): pl.pallas_call(hand_over, out_shape=(jax.ShapeDtypeStruct(attended.shape,...]
where the time goes in v4:
time: 148 us
  Pallas kernels  147 us (99%)
    pallas_call x1, Pallas kernels, per_device(): pl.pallas_call(kernel, out_shape=(jax.ShapeDtypeStruct((ROUNDS, Y, 2, 64,...  145 us

profile of v4, /device:TPU:1, one launch (start us, length us, event | category | flops | bytes accessed | tf_op | source)
XLA Modules:
  0.0 148.3 jit_solution(1197506492421279911)
XLA Ops:
  1.3 144.6 %attend_and_project.1 = (bf16[2,4,2,64,512]{4,3,2,1,0:T(8,128)(2,1)}, bf16[2,64,4096]{2,1,0:T(8,128)(2,1)}) custom-call(s32[2,3,1,4]{3,2,1,0:T(1,128)} %bitcast.3, s32[1]{0:T(128)S(6)} %copy.8.len_ref, bf16[2,512,512]{2,1,0:T(8,128)(2,1)} %q_ref.1, bf16[2,512,128]{2,1,0:T(8,128)(2,1)} %k_ref.1, bf16[2,512,128]{2,1,0:T(8,128)(2,1)} %v_ref.1, ...), custom_call_target="tpu_custom_call" | custom-call | flops 9663676416 | bytes 8388608 | tf_op jit(solution)/shard_map/attend_and_project/pallas_call | solution.py:550
  145.9 2.4 %hand_over.1 = (bf16[2,512,512]{2,1,0:T(8,128)(2,1)}, bf16[2,64,4096]{2,1,0:T(8,128)(2,1)}) custom-call(bf16[2,512,512]{2,1,0:T(8,128)(2,1)} %bitcast.2, bf16[2,64,4096]{2,1,0:T(8,128)(2,1)} %get-tuple-element.5.out_in), custom_call_target="tpu_custom_call" | custom-call | tf_op jit(solution)/shard_map/hand_over/pallas_call | solution.py:603

commit v5 on v4

--- a/solution.py
+++ b/solution.py
@@ -216,17 +216,30 @@
                 def _():
                     act(copy_b(r, hi, down, sbz.at[r, hi]))
 
-    def far_tile(r, block):
-        query_t = qt.at[tile_of[block]]
-        newer = round_of[block] == 1
-        key_tile = jnp.where(newer, kv[r, block, 0], kv[0, block, 0])
-        value_t = value_rows(jnp.where(newer, kv[r, block, 1], kv[0, block, 1]))
-        for c in range(2):
-            cols = slice(c * 256, (c + 1) * 256)
-            mixed, highest, total = soft_part(key_tile, value_t, query_t[:, cols])
-            us[block, :, cols] = mixed
+    def far_tiles(r, blocks):
+        def scores_of(block, cols):
+            newer = round_of[block] == 1
+            key_tile = jnp.where(newer, kv[r, block, 0], kv[0, block, 0])
+            query_t = qt[tile_of[block], :, cols]
+            return jnp.dot(key_tile, query_t, preferred_element_type=jnp.float32)
+
+        def mix(block, cols, scores):
+            newer = round_of[block] == 1
+            value_t = value_rows(jnp.where(newer, kv[r, block, 1], kv[0, block, 1]))
+            highest = jnp.max(scores, axis=0, keepdims=True)
+            weights = jnp.exp2((scores - highest) * GAIN)
             ms[block, :, cols] = highest
-            ls[block, :, cols] = total
+            ls[block, :, cols] = jnp.sum(weights, axis=0, keepdims=True)
+            us[block, :, cols] = jnp.dot(
+                value_t, weights.astype(jnp.bfloat16), preferred_element_type=jnp.float32
+            )
+
+        parts = [(block, slice(c * 256, (c + 1) * 256)) for block in blocks for c in range(2)]
+        scores = scores_of(*parts[0])
+        for i, part_now in enumerate(parts):
+            ahead = scores_of(*parts[i + 1]) if i + 1 < len(parts) else None
+            mix(*part_now, scores)
+            scores = ahead
 
     def own_tile(r, h):
         tile = r * HEADS + h
@@ -245,9 +258,14 @@
     def far_slots(r, k, off):
         inner, is_below = inner_of(k), below(r, k)
 
-        def one(side, carry):
-            zz = jnp.where(side == 0, z + Z - k, z + k)
-            block = at(zz, x + off)
+        def block_of(side):
+            return at(jnp.where(side == 0, z + Z - k, z + k), x + off)
+
+        def useful(side):
+            live = jnp.logical_or(side == 0, inner)
+            return jnp.logical_and(live, jnp.logical_or(r == 0, block_of(side) < seq))
+
+        def arrive(side, carry):
             from_left = jnp.where(inner, side == 0, is_below)
             live = jnp.logical_or(side == 0, inner)
             pending = jnp.logical_or(
@@ -260,15 +278,27 @@
 
             @pl.when(jnp.logical_and(live, pending))
             def _():
-                wait_a(r, block)
-
-            @pl.when(jnp.logical_and(live, jnp.logical_or(r == 0, block < seq)))
-            def _():
-                far_tile(r, block)
+                wait_a(r, block_of(side))
 
             return carry
 
-        lax.fori_loop(0, 2, one, 0)
+        lax.fori_loop(0, 2, arrive, 0)
+        both = jnp.logical_and(useful(0), useful(1))
+
+        @pl.when(both)
+        def _():
+            far_tiles(r, (block_of(0), block_of(1)))
+
+        @pl.when(jnp.logical_not(both))
+        def _():
+            def one(side, carry):
+                @pl.when(useful(side))
+                def _():
+                    far_tiles(r, (block_of(side),))
+
+                return carry
+
+            lax.fori_loop(0, 2, one, 0)
 
     def copy_att(r, h):
         return pltpu.make_async_remote_copy(

time: 148 us -> 140 us (0.946)
  Pallas kernels: 147 us -> 138 us
    pallas_call x1, Pallas kernels: 145 us -> 136 us  [per_device(): pl.pallas_call(kernel, out_shape=(jax.ShapeDtypeStruct((ROUNDS, Y, 2, 64,...]
where the time goes in v5:
time: 140 us; the launch traced here: 139 us
  Pallas kernels  138 us (99%)
    pallas_call x1, Pallas kernels, per_device(): pl.pallas_call(kernel, out_shape=(jax.ShapeDtypeStruct((ROUNDS, Y, 2, 64,...  136 us

profile of v5, /device:TPU:1, one launch (start us, length us, event | category | flops | bytes accessed | tf_op | source)
XLA Modules:
  0.0 139.4 jit_solution(12501156040540086140)
XLA Ops:
  1.3 135.7 %attend_and_project.1 = (bf16[2,4,2,64,512]{4,3,2,1,0:T(8,128)(2,1)}, bf16[2,64,4096]{2,1,0:T(8,128)(2,1)}) custom-call(s32[2,3,1,4]{3,2,1,0:T(1,128)} %bitcast.3, s32[1]{0:T(128)S(6)} %copy.8.len_ref, bf16[2,512,512]{2,1,0:T(8,128)(2,1)} %q_ref.1, bf16[2,512,128]{2,1,0:T(8,128)(2,1)} %k_ref.1, bf16[2,512,128]{2,1,0:T(8,128)(2,1)} %v_ref.1, ...), custom_call_target="tpu_custom_call" | custom-call | flops 9663676416 | bytes 8388608 | tf_op jit(solution)/shard_map/attend_and_project/pallas_call | solution.py:580
  137.0 2.4 %hand_over.1 = (bf16[2,512,512]{2,1,0:T(8,128)(2,1)}, bf16[2,64,4096]{2,1,0:T(8,128)(2,1)}) custom-call(bf16[2,512,512]{2,1,0:T(8,128)(2,1)} %bitcast.2, bf16[2,64,4096]{2,1,0:T(8,128)(2,1)} %get-tuple-element.5.out_in), custom_call_target="tpu_custom_call" | custom-call | tf_op jit(solution)/shard_map/hand_over/pallas_call | solution.py:633

commit v6 on v5

--- a/solution.py
+++ b/solution.py
@@ -21,32 +21,19 @@
 MESH = pl.DeviceIdType.MESH
 STEPS = 104
 FORWARD = (
-    4989827, 8718083, 0, 9381394, 8914067, 49, 42729747, 26531,
-    3294785, 91661, 114066482, 17720832, 103546905, 36438016, 118248259, 99867,
-    70202880, 79386, 57, 74405419, 87562, 15488073, 15431168, 0,
-    78418944, 19895995, 53376512, 169472, 0, 0, 0, 0,
+    4457859, 5113475, 4793889, 206336, 72107008, 9200291, 3360547, 6721,
+    114058240, 80504499, 36450816, 103777819, 51118146, 17729034, 10747904, 13579,
+    155, 107741184, 11301376, 112080384, 11047595, 0, 153147, 58,
+    116167680, 95744, 82575435, 104395, 331, 0, 0, 0,
     0, 0, 0,
 )
 WORK = (
-    0, 6815744, 15229962, 0, 8650752, 105129345, 17425, 42206208,
-    33816625, 67584512, 71565601, 17039505, 11231745, 103178929, 9, 84247489,
-    17923, 6563379, 5245337, 9437184, 73689088, 5722624, 10834569, 115634953,
-    40110645, 119799993, 52843081, 3052345, 7099963, 7346213, 7632940, 3435565,
-    9972742, 12074045, 31758,
+    8912896, 0, 524314, 67379754, 15278593, 0, 100925449, 71771041,
+    33833482, 4718592, 82609, 103022881, 25905, 35913728, 221761, 117727744,
+    5079873, 922147, 5244979, 36, 44302388, 40127017, 111421952, 9974329,
+    115605913, 48524057, 77894149, 82154441, 2905929, 3159611, 11562012, 3411004,
+    3701277, 5782573, 23614,
 )
-
-
-def soft_part(key_tile, value_t, query_t, mask_from=None):
-    scores = jnp.dot(key_tile, query_t, preferred_element_type=jnp.float32)
-    if mask_from is not None:
-        key_at = lax.broadcasted_iota(jnp.int32, scores.shape, 0)
-        query_at = lax.broadcasted_iota(jnp.int32, scores.shape, 1) + mask_from
-        scores = jnp.where(key_at <= query_at, scores, -1e30)
-    highest = jnp.max(scores, axis=0, keepdims=True)
-    weights = jnp.exp2((scores - highest) * GAIN)
-    total = jnp.sum(weights, axis=0, keepdims=True)
-    mixed = jnp.dot(value_t, weights.astype(jnp.bfloat16), preferred_element_type=jnp.float32)
-    return mixed, highest, total
 
 
 def value_rows(stacked):
@@ -56,7 +43,7 @@
 def kernel(
     sel_ref, len_ref, q_ref, k_ref, v_ref, w_ref,
     att_ref, out_ref,
-    kv, qv, vv, qt, us, ms, ls, wo, ws, attx, sib, part, relay, fin, outv, tile_of, round_of,
+    kv, qv, vv, qt, us, ms, ls, ww, attx, sib, part, relay, fin, outv, tile_of, round_of,
     ra, rb, saz, sax, sbx, sbz, insem, wsem, att_s, att_r, rs_s, relay_r, fin_r, att_o, out_o,
 ):
     seq = lax.axis_index("seq")
@@ -73,22 +60,22 @@
     back = lax.rem(y + 3, Y) * 2 + core
     twin = y * 2 + 1 - core
 
+    load_v = pltpu.make_async_copy(v_ref, vv, insem.at[0])
+    load_k = [
+        pltpu.make_async_copy(k_ref.at[r], kv.at[r, seq, 0], insem.at[1 + r]) for r in range(ROUNDS)
+    ]
+    load_q = pltpu.make_async_copy(q_ref, qv, insem.at[3])
+    load_w = pltpu.make_async_copy(w_ref, ww.at[0], wsem.at[2])
+    load_v.start()
+    for load in load_k:
+        load.start()
+    load_q.start()
     barrier = pltpu.get_barrier_semaphore()
     for peer in (up, down, right, left):
         pl.semaphore_signal(barrier, inc=1, device_id={"seq": peer}, device_id_type=MESH)
     for peer in (front, back, twin):
         pl.semaphore_signal(barrier, inc=1, device_id={"head": peer}, device_id_type=MESH)
 
-    load_v = pltpu.make_async_copy(v_ref, vv, insem.at[0])
-    load_k = [
-        pltpu.make_async_copy(k_ref.at[r], kv.at[r, seq, 0], insem.at[1 + r]) for r in range(ROUNDS)
-    ]
-    load_q = pltpu.make_async_copy(q_ref, qv, insem.at[3])
-    load_w = pltpu.make_async_copy(w_ref, wo, wsem.at[2])
-    load_v.start()
-    for load in load_k:
-        load.start()
-    load_q.start()
     load_v.wait()
     for r in range(ROUNDS):
         for c in range(4):
@@ -245,15 +232,27 @@
         tile = r * HEADS + h
         key_tile = kv[r, seq, 0]
         value_t = value_rows(kv[r, seq, 1])
+        parts = []
         for c in range(2):
             cols = slice(c * 256, (c + 1) * 256)
             keys_to = (c + 1) * 256
-            mixed, highest, total = soft_part(
-                key_tile[:keys_to], value_t[:, :keys_to], qt[tile, :, cols], c * 256
+            scores = jnp.dot(
+                key_tile[:keys_to], qt[tile, :, cols], preferred_element_type=jnp.float32
             )
-            us[PEERS + tile, :, cols] = mixed
+            parts.append((cols, keys_to, scores))
+        for cols, keys_to, scores in parts:
+            key_at = lax.broadcasted_iota(jnp.int32, scores.shape, 0)
+            query_at = lax.broadcasted_iota(jnp.int32, scores.shape, 1) + (keys_to - 256)
+            scores = jnp.where(key_at <= query_at, scores, -1e30)
+            highest = jnp.max(scores, axis=0, keepdims=True)
+            weights = jnp.exp2((scores - highest) * GAIN)
             ms[PEERS + tile, :, cols] = highest
-            ls[PEERS + tile, :, cols] = total
+            ls[PEERS + tile, :, cols] = jnp.sum(weights, axis=0, keepdims=True)
+            us[PEERS + tile, :, cols] = jnp.dot(
+                value_t[:, :keys_to],
+                weights.astype(jnp.bfloat16),
+                preferred_element_type=jnp.float32,
+            )
 
     def far_slots(r, k, off):
         inner, is_below = inner_of(k), below(r, k)
@@ -346,7 +345,7 @@
 
     def copy_w():
         return pltpu.make_async_remote_copy(
-            src_ref=w_ref, dst_ref=ws, send_sem=wsem.at[0], recv_sem=wsem.at[1],
+            src_ref=w_ref, dst_ref=ww.at[1], send_sem=wsem.at[0], recv_sem=wsem.at[1],
             device_id={"head": twin}, device_id_type=MESH,
         )
 
@@ -368,16 +367,13 @@
         )
 
     def project(r, n):
-        own_rows = jnp.concatenate(
-            [attx[r, core, h].reshape(Y * 64, HEAD) for h in range(HEADS)], axis=1
-        )
-        twin_rows = jnp.concatenate(
-            [sib[r, h].reshape(Y * 64, HEAD) for h in range(HEADS)], axis=1
-        )
+        rows = [attx[r, core, h].reshape(Y * 64, HEAD) for h in range(HEADS)]
+        rows += [sib[r, h].reshape(Y * 64, HEAD) for h in range(HEADS)]
+        rows = jnp.concatenate(rows, axis=1)
         for half in range(2):
             cols = pl.ds(pl.multiple_of(n * COLS + half * HALF, HALF), HALF)
-            term = jnp.dot(own_rows, wo[:, cols], preferred_element_type=jnp.float32)
-            term = term + jnp.dot(twin_rows, ws[:, cols], preferred_element_type=jnp.float32)
+            weight = ww[:, :, cols].reshape(2 * HEADS * HEAD, HALF)
+            term = jnp.dot(rows, weight, preferred_element_type=jnp.float32)
             part[r, n, :, half] = term.astype(jnp.bfloat16).reshape(Y, 64, HALF)
         copy_relay(r, n, 0).start()
         copy_relay(r, n, 1).start()
@@ -593,8 +589,7 @@
             pltpu.VMEM((PEERS + ROUNDS * HEADS, HEAD, BLOCK), f32),
             pltpu.VMEM((PEERS + ROUNDS * HEADS, 1, BLOCK), f32),
             pltpu.VMEM((PEERS + ROUNDS * HEADS, 1, BLOCK), f32),
-            pltpu.VMEM((HEADS * HEAD, MODEL), bf16),
-            pltpu.VMEM((HEADS * HEAD, MODEL), bf16),
+            pltpu.VMEM((2, HEADS * HEAD, MODEL), bf16),
             pltpu.VMEM((ROUNDS, 2, HEADS, Y, 64, HEAD), bf16),
             pltpu.VMEM((ROUNDS, HEADS, Y, 64, HEAD), bf16),
             pltpu.VMEM((ROUNDS, TILES, Y, 2, 64, HALF), bf16),

time: 140 us -> 139 us (level)
  no operation moved by 1% of the time
where the time goes in v6:
time: 139 us
  Pallas kernels  138 us (99%)
    pallas_call x1, Pallas kernels, per_device(): pl.pallas_call(kernel, out_shape=(jax.ShapeDtypeStruct((ROUNDS, Y, 2, 64,...  135 us

profile of v6, /device:TPU:1, one launch (start us, length us, event | category | flops | bytes accessed | tf_op | source)
XLA Modules:
  0.0 139.1 jit_solution(2838475821369601149)
XLA Ops:
  1.3 135.4 %attend_and_project.1 = (bf16[2,4,2,64,512]{4,3,2,1,0:T(8,128)(2,1)}, bf16[2,64,4096]{2,1,0:T(8,128)(2,1)}) custom-call(s32[2,3,1,4]{3,2,1,0:T(1,128)} %bitcast.3, s32[1]{0:T(128)S(6)} %copy.8.len_ref, bf16[2,512,512]{2,1,0:T(8,128)(2,1)} %q_ref.1, bf16[2,512,128]{2,1,0:T(8,128)(2,1)} %k_ref.1, bf16[2,512,128]{2,1,0:T(8,128)(2,1)} %v_ref.1, ...), custom_call_target="tpu_custom_call" | custom-call | flops 9663676416 | bytes 8388608 | tf_op jit(solution)/shard_map/attend_and_project/pallas_call | solution.py:576
  136.7 2.4 %hand_over.1 = (bf16[2,512,512]{2,1,0:T(8,128)(2,1)}, bf16[2,64,4096]{2,1,0:T(8,128)(2,1)}) custom-call(bf16[2,512,512]{2,1,0:T(8,128)(2,1)} %bitcast.2, bf16[2,64,4096]{2,1,0:T(8,128)(2,1)} %get-tuple-element.5.out_in), custom_call_target="tpu_custom_call" | custom-call | tf_op jit(solution)/shard_map/hand_over/pallas_call | solution.py:628

commit v7 on v6

--- a/solution.py
+++ b/solution.py
@@ -19,20 +19,20 @@
 HALF = COLS // 2
 TILES = MODEL // COLS
 MESH = pl.DeviceIdType.MESH
-STEPS = 104
+STEPS = 100
 FORWARD = (
     4457859, 5113475, 4793889, 206336, 72107008, 9200291, 3360547, 6721,
     114058240, 80504499, 36450816, 103777819, 51118146, 17729034, 10747904, 13579,
-    155, 107741184, 11301376, 112080384, 11047595, 0, 153147, 58,
-    116167680, 95744, 82575435, 104395, 331, 0, 0, 0,
-    0, 0, 0,
+    155, 15152640, 74186795, 19224491, 42, 78411264, 29696, 19398656,
+    49021371, 38400, 53450555, 169472, 0, 0, 0, 0,
+    0, 0,
 )
 WORK = (
     8912896, 0, 524314, 67379754, 15278593, 0, 100925449, 71771041,
     33833482, 4718592, 82609, 103022881, 25905, 35913728, 221761, 117727744,
-    5079873, 922147, 5244979, 36, 44302388, 40127017, 111421952, 9974329,
-    115605913, 48524057, 77894149, 82154441, 2905929, 3159611, 11562012, 3411004,
-    3701277, 5782573, 23614,
+    9274177, 1050377, 18452, 26624, 9720489, 5505177, 6583209, 209446,
+    14037945, 19139257, 52925225, 11440953, 7346187, 15751222, 7608838, 11803709,
+    16264222, 46,
 )
 
 
@@ -336,7 +336,7 @@
         mixed = us[own] * (weights[0] * norm)
         for slot, weight in zip(slots, weights[1:]):
             mixed = mixed + us[slot] * (weight * norm)
-        rows = mixed.T.astype(jnp.bfloat16).reshape(Y, 2, 64, HEAD)
+        rows = mixed.astype(jnp.bfloat16).T.reshape(Y, 2, 64, HEAD)
         for c in range(2):
             attx[r, c, h] = rows[:, c]
         copy_att(r, h).start()
@@ -478,6 +478,7 @@
         @pl.when(work == 3)
         def _():
             merge(wr, item)
+            merge(wr, item + 1)
 
         @pl.when(work == 4)
         def _():

time: 139 us -> 139 us (level)
  no operation moved by 1% of the time
where the time goes in v7:
time: 139 us
  Pallas kernels  138 us (99%)
    pallas_call x1, Pallas kernels, per_device(): pl.pallas_call(kernel, out_shape=(jax.ShapeDtypeStruct((ROUNDS, Y, 2, 64,...  135 us

profile of v7, /device:TPU:1, one launch (start us, length us, event | category | flops | bytes accessed | tf_op | source)
XLA Modules:
  0.0 138.8 jit_solution(18320542031259105642)
XLA Ops:
  1.3 135.2 %attend_and_project.1 = (bf16[2,4,2,64,512]{4,3,2,1,0:T(8,128)(2,1)}, bf16[2,64,4096]{2,1,0:T(8,128)(2,1)}) custom-call(s32[2,3,1,4]{3,2,1,0:T(1,128)} %bitcast.3, s32[1]{0:T(128)S(6)} %copy.8.len_ref, bf16[2,512,512]{2,1,0:T(8,128)(2,1)} %q_ref.1, bf16[2,512,128]{2,1,0:T(8,128)(2,1)} %k_ref.1, bf16[2,512,128]{2,1,0:T(8,128)(2,1)} %v_ref.1, ...), custom_call_target="tpu_custom_call" | custom-call | flops 9663676416 | bytes 8388608 | tf_op jit(solution)/shard_map/attend_and_project/pallas_call | solution.py:577
  136.4 2.4 %hand_over.1 = (bf16[2,512,512]{2,1,0:T(8,128)(2,1)}, bf16[2,64,4096]{2,1,0:T(8,128)(2,1)}) custom-call(bf16[2,512,512]{2,1,0:T(8,128)(2,1)} %bitcast.2, bf16[2,64,4096]{2,1,0:T(8,128)(2,1)} %get-tuple-element.5.out_in), custom_call_target="tpu_custom_call" | custom-call | tf_op jit(solution)/shard_map/hand_over/pallas_call | solution.py:629
